TPU v7x, 256 devices: a whole 4x4x8 slice. The times are simulated.
256 devices in a mesh: source: 32 (over z, y), row: 4 (over x), cond: 2 (over core).
Axes of the slice: x: 4, y: 4, z: 8, core: 2. Of those that a mesh axis runs over, the one named last changes fastest.
Arguments:
- spectrum: bfloat16 [2, 1024, 1024], P(None, ('source', 'row')), may hold values from -0.046875 to 0.046875
- centers: float32 [32, 2], P('source'), may hold values from 0 to 1024
- blocks: int32 [32, 8], P('source'), may hold values from 0 to 63, as said below
- counts: int32 [32], P('source'), may hold values from 1 to 8
- weights: float32 [32], P('source'), may hold values from 0.2 to 1
- defocus: float32 [4], P('cond'), may hold values from -3 to 3
- dose_scale: float32 [4], P('cond'), may hold values from 0.5 to 2
Outputs:
- soft_slope: float32 [512, 4096], P('row', 'source')
Inputs may be any that keep to these rules, and one draw needn't show every extreme that they name: `blocks`: the entries of one row are distinct block numbers; entries of row s past counts[s] are not used.
All inputs are finite; a program needn't handle non-finite values.
Results may differ from a plain program's by a relative error of at most 0.00035.
The roundings to bfloat16 on the way count: a program that leaves them out, or rounds other values in their place, can miss the bound.
Values may be sent and summed in bfloat16 or wider, within the bound.
No kernel may reach another device: no remote copies, remote signals or barrier semaphores. Data moves between devices by JAX's collectives and lax.ppermute only.
A program may use at most 64 MiB of HBM per device.

v0:
```python
import functools
import math

import jax
import jax.numpy as jnp
from jax import lax
from jax.experimental import pallas as pl
from jax.experimental.pallas import tpu as pltpu
from jax.sharding import PartitionSpec as P

N = 4096
BLOCK = 128
NB = 8
XR = 128
SPEC = 1024
SOURCES = 32
SLOTS = 8
CONDS = 4
W = 64
ROWS = 72
PART = 32
PART_ROWS = 40
GROUP = 4
LOCAL = SOURCES // 2
ENTRIES = LOCAL * SLOTS

TAU = 0.5
BACKGROUND = 0.05

F32 = jnp.float32
BF16 = jnp.bfloat16

TILE_GROUPS = [[8 * k + t for k in range(4) for t in (q, 7 - q)] for q in range(4)]


def phases(product):
    angle = jnp.mod(product, N).astype(F32) * (2.0 * math.pi / N)
    return jnp.cos(angle).astype(BF16), jnp.sin(angle).astype(BF16)


def spread(value, axis, count):
    copies = jnp.broadcast_to(value[None], (count,) + value.shape)
    return lax.all_to_all(copies, axis, 0, 0)


def round_bf16(value):
    return lax.reduce_precision(value, 8, 7)


def turn_kernel(rows_ref, select_ref, out_ref):
    for j in range(4):
        parts = [
            rows_ref[n % 4, n // 4, :, 128 * j:128 * j + 128].astype(F32) for n in range(16)
        ]
        stack = jnp.concatenate([p[:8] for p in parts] + [p[8:] for p in parts], axis=0).astype(BF16)
        done = lax.dot_general(
            select_ref[...], stack, (((1,), (1,)), ((), ())), preferred_element_type=F32
        )
        out_ref[0, j] = done.astype(BF16)


def image_kernel(
    total_ref, home_ref, slot_ref, block_ref, i_ref, j_ref, weight_ref, core_ref,
    own_ref, other_ref, p_ref, q_ref, rowf_ref, colf_ref,
    keep_ref, send_ref, turned, pieces, power, sems,
):
    copies = [
        pltpu.make_async_copy(ref, turned.at[pl.ds(32 * n, 32)], sems.at[n])
        for n, ref in enumerate((own_ref, other_ref))
    ]
    for copy in copies:
        copy.start()
    pieces[...] = jnp.zeros_like(pieces)
    power[...] = jnp.zeros_like(power)
    for copy in copies:
        copy.wait()

    def entries(g, carry):
        p_all = p_ref[g]
        q_all = jnp.transpose(q_ref[g])
        for n in range(GROUP):
            t = g * GROUP + n
            block = turned[block_ref[t]].astype(F32)
            re, im = block[:, :128], block[:, 128:]
            pr, pi = p_all[2 * n:2 * n + 1], p_all[2 * n + 1:2 * n + 2]
            qr, qi = q_all[:, 2 * n:2 * n + 1], q_all[:, 2 * n + 1:2 * n + 2]
            pupil_re = qr * pr - qi * pi
            pupil_im = qr * pi + qi * pr
            masked_re = (re * pupil_re - im * pupil_im).astype(BF16)
            masked_im = (re * pupil_im + im * pupil_re).astype(BF16)
            masked = jnp.concatenate([masked_re, masked_im], axis=1)
            piece = jnp.dot(masked, rowf_ref[i_ref[t]], preferred_element_type=F32).astype(BF16)
            place = pl.ds(pl.multiple_of(32 * slot_ref[t], 32), 32)
            for r in range(4):
                pieces[home_ref[t], r, place, :] = piece[32 * r:32 * r + 32]
        return carry

    lax.fori_loop(0, (total_ref[0] + GROUP - 1) // GROUP, entries, 0)

    lane_group = lax.broadcasted_iota(jnp.int32, (2 * ROWS, 128), 1) // 32

    def fields(s, carry):
        direct, mirror = [], []
        for r in range(4):
            halves = []
            for h in range(2):
                table = None
                for m in range(4):
                    term = colf_ref[j_ref[s * SLOTS + 4 * h + m], (m - r) % 4]
                    table = term if table is None else jnp.where(lane_group == m, term, table)
                halves.append(table)
            table = jnp.concatenate(halves, axis=1)
            both = jnp.dot(table, pieces[s, r], preferred_element_type=F32)
            a_cos, b_cos = both[:ROWS, :128], both[:ROWS, 128:]
            a_sin, b_sin = both[ROWS:, :128], both[ROWS:, 128:]
            direct.append((a_cos - b_sin, a_sin + b_cos))
            mirror.append((a_cos + b_sin, b_cos - a_sin))
        weight = weight_ref[s]
        for base, parts in ((0, direct), (4, mirror)):
            (r0, i0), (r1, i1), (r2, i2), (r3, i3) = parts
            gr, gi, dr, di = r0 + r2, i0 + i2, r0 - r2, i0 - i2
            hr, hi, er, ei = r1 + r3, i1 + i3, r1 - r3, i1 - i3
            images = ((gr + hr, gi + hi), (dr - ei, di + er), (gr - hr, gi - hi), (dr + ei, di - er))
            for m, (fr, fi) in enumerate(images):
                power[base + m] += weight * (fr * fr + fi * fi)
        return carry

    lax.fori_loop(0, LOCAL, fields, 0)
    mine = pl.multiple_of(PART * core_ref[0], PART)
    theirs = pl.multiple_of(PART * (1 - core_ref[0]), PART)
    for image in range(8):
        keep_ref[image] = power[image, pl.ds(mine, PART_ROWS), :]
        send_ref[image] = power[image, pl.ds(theirs, PART_ROWS), :]


def slope_kernel(dose_ref, keep_ref, other_ref, out_ref):
    dose = dose_ref[0]
    for e in range(8):
        image = e // 2 if e % 2 == 0 else 4 + (e // 2 + 1) % 4
        low = 1 + e % 2
        level = dose * (keep_ref[image] + other_ref[image]) / SOURCES + BACKGROUND
        slope = jnp.abs(level[low + 1:low + 1 + PART] - level[low - 1:low - 1 + PART]) / (
            2.0 * level[low:low + PART]
        )
        out_ref[e] = jnp.exp(slope * (-1.0 / TAU))


def on_device(spectrum, centers, blocks, counts, weights, defocus, dose_scale):
    core = lax.axis_index("cond")
    source = lax.axis_index("source")
    z, y = source // 4, source % 4
    swap = [(0, 1), (1, 0)]
    half = lax.dynamic_slice(spectrum, (0, 0, 512 * core), (2, 8, 512)).reshape(16, 512)
    info = jnp.concatenate(
        [centers, counts.astype(F32)[:, None], weights[:, None], blocks.astype(F32)], axis=1
    )
    high = round_bf16(info)
    mid = round_bf16(info - high)
    low = round_bf16(info - high - mid)
    info = jnp.concatenate([high, mid, low], axis=0).astype(BF16)
    info = jnp.pad(info, ((0, 13), (0, 116)))
    column = spread(jnp.concatenate([half, info], axis=1), "source", 32)
    rows = spread(column[:, :, :512], "row", 4)

    local = jnp.concatenate([defocus, dose_scale])
    remote = lax.ppermute(local, "cond", swap)
    cond = z % 4
    chosen = jnp.where(cond // 2 == core, local, remote)
    focus = jnp.where(cond % 2 == 0, chosen[0], chosen[1])
    dose = jnp.where(cond % 2 == 0, chosen[2], chosen[3])
    quarter = jnp.where(z % 2 == 0, y, 3 - y)
    window = 2 * quarter + z // 4

    info = column[:, :3, 512:524].astype(F32)
    info = info[:, 0] + info[:, 1] + info[:, 2]
    number = jnp.arange(SOURCES, dtype=jnp.int32)
    used = info[:, 2]
    before = (used[None, :] > used[:, None]) | (
        (used[None, :] == used[:, None]) & (number[None, :] < number[:, None])
    )
    rank = jnp.sum(before.astype(jnp.int32), axis=1)
    position = jnp.arange(LOCAL, dtype=jnp.int32)
    wanted = 4 * (position // 2) + jnp.where(position % 2 == 0, core, 3 - core)
    picked = jnp.where(rank[None, :, None] == wanted[:, None, None], info[None], 0.0)
    info = jnp.sum(picked, axis=1)
    used = info[:, 2].astype(jnp.int32)
    listing = info[:, 4:12].astype(jnp.int32)
    start = jnp.sum(jnp.where(position[None, :] < position[:, None], used[None, :], 0), axis=1)
    total = jnp.sum(used)
    entry = jnp.arange(ENTRIES, dtype=jnp.int32)
    inside = (entry[:, None] >= start[None, :]) & (entry[:, None] < (start + used)[None, :])
    home = LOCAL - jnp.sum(jnp.where(inside, LOCAL - position[None, :], 0), axis=1)
    slot = jnp.sum(jnp.where(inside, entry[:, None] - start[None, :], 0), axis=1)
    center = jnp.sum(jnp.where(inside[:, :, None], info[None, :, :2], 0.0), axis=1)
    slots = jnp.arange(SLOTS, dtype=jnp.int32)
    chosen = inside[:, :, None] & (slots[None, None, :] == slot[:, None, None])
    number = jnp.sum(jnp.where(chosen, listing[None], 0), axis=(1, 2))
    row_block, col_block = number // NB, number % NB
    block = ((col_block // 4) ^ core) * 32 + row_block * 4 + col_block % 4
    col_list = jnp.where(slots[None, :] < used[:, None], listing % NB, NB)

    offsets = jnp.arange(BLOCK, dtype=jnp.int32)
    by_residue = (offsets % 32) * 4 + offsets // 32

    def pupil_factor(number, inner, center):
        gap = (number[:, None] * BLOCK + inner[None, :]).astype(F32) - center[:, None]
        radius = gap * gap / (4.0 * BLOCK * BLOCK)
        amplitude = jnp.exp(-radius)
        angle = focus * radius
        parts = jnp.stack([amplitude * jnp.cos(angle), amplitude * jnp.sin(angle)], axis=1)
        return parts.reshape(ENTRIES // GROUP, 2 * GROUP, BLOCK)

    p_all = pupil_factor(row_block, offsets, center[:, 0])
    q_all = pupil_factor(col_block, by_residue, center[:, 1])

    image_rows = lax.axis_index("row") * XR + jnp.arange(XR, dtype=jnp.int32)
    spec_index = jnp.arange(SPEC, dtype=jnp.int32) - SPEC // 2
    row_cos, row_sin = phases(spec_index[:, None] * image_rows[None, :])
    row_cos, row_sin = row_cos.reshape(NB, BLOCK, XR), row_sin.reshape(NB, BLOCK, XR)
    rowf = jnp.concatenate(
        [jnp.concatenate([row_cos, row_sin], axis=2), jnp.concatenate([-row_sin, row_cos], axis=2)], axis=1
    )

    columns = window * W - 1 + jnp.arange(ROWS, dtype=jnp.int32)
    v_index = (jnp.arange(NB, dtype=jnp.int32)[:, None] * BLOCK + by_residue[None, :]) - SPEC // 2
    col_cos, col_sin = phases(v_index[:, None, :] * columns[None, :, None])
    col = jnp.concatenate([col_cos, col_sin], axis=1)
    col = jnp.pad(col, ((0, 1), (0, 0), (0, 0)))
    colf = jnp.stack(
        [col] + [jnp.concatenate([col[:, :, 128 - 32 * d:], col[:, :, :128 - 32 * d]], axis=2) for d in (1, 2, 3)],
        axis=1,
    )
    select = (by_residue[:, None] == offsets[None, :]).astype(BF16)

    own = pl.pallas_call(
        turn_kernel,
        grid=(8,),
        out_shape=jax.ShapeDtypeStruct((8, 4, 128, 256), BF16),
        in_specs=[
            pl.BlockSpec((4, 4, 16, 512), lambda i: (0, i, 0, 0)),
            pl.BlockSpec((128, 128), lambda i: (0, 0)),
        ],
        out_specs=pl.BlockSpec((1, 4, 128, 256), lambda i: (i, 0, 0, 0)),
    )(rows, select)
    own = own.reshape(32, 128, 256)
    other = lax.ppermute(own, "cond", swap)

    vmem = pl.BlockSpec(memory_space=pltpu.VMEM)
    smem = pl.BlockSpec(memory_space=pltpu.SMEM)
    hbm = pl.BlockSpec(memory_space=pl.ANY)
    keep, send = pl.pallas_call(
        image_kernel,
        out_shape=[jax.ShapeDtypeStruct((8, PART_ROWS, XR), F32)] * 2,
        in_specs=[smem] * 8 + [hbm] * 2 + [vmem] * 4,
        out_specs=[vmem] * 2,
        scratch_shapes=[
            pltpu.VMEM((64, 128, 256), BF16),
            pltpu.VMEM((LOCAL + 1, 4, 256, 256), BF16),
            pltpu.VMEM((8, ROWS, XR), F32),
            pltpu.SemaphoreType.DMA((2,)),
        ],
        compiler_params=pltpu.CompilerParams(vmem_limit_bytes=40 * 1024 * 1024),
    )(
        total.reshape(1), home, slot, block, row_block, col_list.reshape(-1), info[:, 3], core.reshape(1),
        own, other, p_all, q_all, rowf, colf,
    )
    received = lax.ppermute(send, "cond", swap)
    terms = pl.pallas_call(
        slope_kernel,
        out_shape=jax.ShapeDtypeStruct((8, PART, XR), F32),
        in_specs=[smem, vmem, vmem],
        out_specs=vmem,
    )(dose.reshape(1), keep, received)
    terms = lax.all_to_all(terms, "source", 0, 0, axis_index_groups=TILE_GROUPS)
    soft = -TAU * jnp.log(jnp.sum(terms.reshape(2, CONDS, PART, XR), axis=1) / CONDS)
    theirs = lax.ppermute(soft, "cond", swap)
    first, second = jnp.where(core == 0, soft, theirs), jnp.where(core == 0, theirs, soft)
    soft = jnp.stack([first, second], axis=1).reshape(2 * W, XR)
    soft = jnp.where(z % 2 == 0, soft, soft[::-1])
    return soft.T


def solution(mesh):
    in_specs = (
        P(None, ("source", "row"), None),
        P("source", None),
        P("source", None),
        P("source"),
        P("source"),
        P("cond"),
        P("cond"),
    )
    out_specs = P("row", "source")
    return jax.shard_map(
        on_device, mesh=mesh, in_specs=in_specs, out_specs=out_specs, check_vma=False
    )
```

profile of v0, /device:TPU:1, one launch (start us, length us, event | category | flops | bytes accessed | tf_op | source)
XLA Modules:
  0.0 121.2 jit_solution(11409193067138376776)
XLA Ops:
  0.0 0.0 copy-start
  0.0 0.8 pad_maximum_fusion.5
  0.8 3.2 %collective-permute-start = (f32[4]{0:T(128)S(1)}, f32[4]{0:T(128)S(1)}, u32[]{:S(2)}, u32[]{:S(2)}) collective-permute-start(f32[4]{0:T(128)S(1)} %pad_maximum_fusion.5), channel_id=1, source_target_pairs={{0,1},{1,0},{2,3},{3,2},{4,5},{5,4},{6,7},{7,6},{8,9},{9,8},{10,11... | collective-permute-start | bytes 56 | tf_op jit(solution)/shard_map/ppermute | solution.py:166
  5.3 0.7 convert_element_type.88
  6.0 0.7 reduce-precision_convert_fusion.1
  6.7 0.0 copy-done
  6.8 0.9 broadcast_in_dim.91
  7.6 9.5 %all-to-all-start = ((bf16[32,16,640]{2,1,0:T(8,128)(2,1)}), bf16[32,16,640]{2,1,0:T(8,128)(2,1)S(1)}, u32[]{:S(2)}, u32[]{:S(2)}) async-start(bf16[32,16,640]{2,1,0:T(8,128)(2,1)} %broadcast_in_dim.91), calls=%async_computation | async-start | bytes 1310720 | tf_op jit(solution)/shard_map/all_to_all | solution.py:43
  17.3 0.1 add_add_fusion
  17.4 1.2 %cosine_convert_fusion.1 = (bf16[8,72,128]{2,1,0:T(8,128)(2,1)S(1)}, bf16[8,72,128]{2,1,0:T(8,128)(2,1)S(1)}) fusion(s32[72]{0:T(128)S(1)} %iota_add_fusion, s32[8,128]{1,0:T(8,128)S(1)} %add_add_fusion), kind=kLoop, calls=%fused_computation.28 | loop fusion | flops 1179648 | bytes 299296 | tf_op jit(solution)/shard_map/convert_element_type | solution.py:38
  18.6 0.1 fusion.37
  18.7 0.2 fusion.38
  18.9 0.2 fusion.40
  19.0 0.2 fusion.39
  19.3 0.2 maximum_bitcast_fusion.1
  19.4 0.4 maximum_bitcast_fusion
  19.8 2.1 %fusion.12 = bf16[8,128,128]{2,1,0:T(8,128)(2,1)S(1)} fusion(s32[128]{0:T(128)S(1)} %iota_add_fusion.1, s32[8,128]{1,0:T(8,128)S(1)} %add_add_fusion.1), kind=kLoop, calls=%fused_computation.48 | loop fusion | flops 2359296 | bytes 266752 | tf_op jit(solution)/shard_map/neg | solution.py:221
  22.0 2.5 %sine_convert_fusion = (bf16[8,128,128]{2,1,0:T(8,128)(2,1)S(1)}, bf16[8,128,128]{2,1,0:T(8,128)(2,1)S(1)}) fusion(s32[128]{0:T(128)S(1)} %iota_add_fusion.1, s32[8,128]{1,0:T(8,128)S(1)} %add_add_fusion.1), kind=kLoop, calls=%fused_computation.16 | loop fusion | flops 2097152 | bytes 528896 | tf_op jit(solution)/shard_map/convert_element_type | solution.py:38
  24.4 0.0 copy-start.6
  24.5 0.0 copy-start.7
  24.5 0.1 maximum_maximum_fusion.rowf_ref
  24.6 0.2 pad_maximum_fusion.colf_ref
  24.8 0.7 fusion.11.select_ref
  25.5 0.0 collective-permute-done
  25.5 0.1 broadcast_select_fusion
  25.6 0.7 fusion.41
  27.4 8.9 %all-to-all-done = bf16[32,16,640]{2,1,0:T(8,128)(2,1)S(1)} async-done(((bf16[32,16,640]{2,1,0:T(8,128)(2,1)}), bf16[32,16,640]{2,1,0:T(8,128)(2,1)S(1)}, u32[]{:S(2)}, u32[]{:S(2)}) %all-to-all-start) | async-done | bytes 655392 | tf_op jit(solution)/shard_map/all_to_all | solution.py:43
  36.3 0.2 slice_reduce_fusion
  36.5 0.1 copy.51
  36.6 0.2 convert_reduce_fusion
  36.8 0.1 broadcast_compare_fusion
  36.9 0.1 select_reduce_fusion
  37.0 0.1 slice.102
  37.1 1.6 %broadcast_in_dim.104 = bf16[4,32,16,512]{3,2,1,0:T(8,128)(2,1)} broadcast(bf16[32,16,512]{2,1,0:T(8,128)(2,1)S(1)} %slice.102), dimensions={1,2,3} | broadcast | bytes 2621440 | tf_op jit(solution)/shard_map/broadcast_in_dim | solution.py:42
  38.6 4.5 %all-to-all-start.1 = ((bf16[4,32,16,512]{3,2,1,0:T(8,128)(2,1)}), bf16[4,32,16,512]{3,2,1,0:T(8,128)(2,1)}, u32[]{:S(2)}, u32[]{:S(2)}) async-start(bf16[4,32,16,512]{3,2,1,0:T(8,128)(2,1)} %broadcast_in_dim.104), calls=%async_computation.1 | async-start | bytes 4194304 | tf_op jit(solution)/shard_map/all_to_all | solution.py:43
  43.1 0.1 copy.52
  43.2 0.1 copy.53
  43.3 0.1 reshape.814.j_ref
  43.4 0.1 select_reduce_fusion.5
  43.5 0.1 select_reduce_fusion.3
  43.6 0.1 fusion.19
  43.7 23.8 %all-to-all-done.1.rows_ref = bf16[4,32,16,512]{3,2,1,0:T(8,128)(2,1)} async-done(((bf16[4,32,16,512]{3,2,1,0:T(8,128)(2,1)}), bf16[4,32,16,512]{3,2,1,0:T(8,128)(2,1)}, u32[]{:S(2)}, u32[]{:S(2)}) %all-to-all-start.1) | async-done | bytes 2097184 | tf_op jit(solution)/shard_map/all_to_all | solution.py:43
  67.5 6.4 %shard_map.73 = bf16[8,4,128,256]{3,2,1,0:T(8,128)(2,1)} custom-call(bf16[4,32,16,512]{3,2,1,0:T(8,128)(2,1)} %all-to-all-done.1.rows_ref, bf16[128,128]{1,0:T(8,128)(2,1)} %fusion.11.select_ref), custom_call_target="tpu_custom_call" | custom-call | tf_op jit(solution)/shard_map/pallas_call | solution.py:235
  73.9 3.0 %collective-permute-start.1 = (bf16[32,128,256]{2,1,0:T(8,128)(2,1)}, bf16[32,128,256]{2,1,0:T(8,128)(2,1)S(1)}, u32[]{:S(2)}, u32[]{:S(2)}) collective-permute-start(bf16[32,128,256]{2,1,0:T(8,128)(2,1)} %bitcast.52), channel_id=1, source_target_pairs={{0,1},{1,0},{2,3},{3,2},{4,5},{5,4},{6,7},{7,6},{8,9},{9,8},{10,11... | collective-permute-start | bytes 6291464 | tf_op jit(solution)/shard_map/ppermute | solution.py:246
  76.8 0.1 select_reduce_fusion.2
  76.9 0.1 select_reduce_fusion.1
  77.1 0.3 cosine_multiply_fusion
  77.4 0.1 copy.55
  77.5 0.3 cosine_multiply_fusion.1
  77.9 0.1 copy.54
  78.0 0.0 copy-done.5
  78.0 0.6 fusion.35
  78.7 2.2 %collective-permute-done.1.other_ref = bf16[32,128,256]{2,1,0:T(8,128)(2,1)S(1)} collective-permute-done((bf16[32,128,256]{2,1,0:T(8,128)(2,1)}, bf16[32,128,256]{2,1,0:T(8,128)(2,1)S(1)}, u32[]{:S(2)}, u32[]{:S(2)}) %collective-permute-start.1) | collective-permute-done | bytes 2097184 | tf_op jit(solution)/shard_map/ppermute | solution.py:246
  80.8 1.6 %copy-done.1 = bf16[8,4,128,256]{3,2,1,0:T(8,128)(2,1)S(1)} copy-done((bf16[8,4,128,256]{3,2,1,0:T(8,128)(2,1)S(1)}, bf16[8,4,128,256]{3,2,1,0:T(8,128)(2,1)}, u32[]{:S(2)}) %copy-start.1) | copy-done | bytes 2097176
  82.4 17.0 %shard_map.74 = (f32[8,40,128]{2,1,0:T(8,128)S(1)}, f32[8,40,128]{2,1,0:T(8,128)S(1)}) custom-call(s32[1]{0:T(128)} %bitcast.7.total_ref, s32[128]{0:T(128)S(1)} %broadcast_subtract_fusion.home_ref, s32[128]{0:T(128)S(1)} %get-tuple-element.9.slot_ref, s32[128]{0:T(128)S(1)} %fusion.28.block_ref, s32[128]{0:T(128)S(1)} %get-tuple-element.14.i_ref, ...), custom_call_target="tpu_custom_call" | custom-call | tf_op jit(solution)/shard_map/pallas_call | solution.py:251
  99.5 0.6 copy-done.2
  100.1 0.9 collective-permute-start.2
  102.3 0.0 collective-permute-done.2.other_ref
  102.3 0.7 copy-done.3
  102.9 1.8 %shard_map.75 = f32[8,32,128]{2,1,0:T(8,128)} custom-call(f32[1]{0:T(128)} %bitcast.2.dose_ref, f32[8,40,128]{2,1,0:T(8,128)} %copy-done.2, f32[8,40,128]{2,1,0:T(8,128)} %copy-done.3), custom_call_target="tpu_custom_call" | custom-call | tf_op jit(solution)/shard_map/pallas_call | solution.py:268
  104.7 12.5 %all_to_all.15 = f32[8,32,128]{2,1,0:T(8,128)S(1)} all-to-all(f32[8,32,128]{2,1,0:T(8,128)} %shard_map.75), channel_id=1, replica_groups={{0,56,64,120,128,184,192,248},{8,48,72,112,136,176,200,240},{16,40,80,1..., dimensions={0} | all-to-all | bytes 262144 | tf_op jit(solution)/shard_map/all_to_all | solution.py:274
  117.2 2.3 %collective-permute-start.3 = (f32[2,32,128]{2,1,0:T(8,128)S(1)}, f32[2,32,128]{2,1,0:T(8,128)S(1)}, u32[]{:S(2)}, u32[]{:S(2)}) collective-permute-start(f32[2,32,128]{2,1,0:T(8,128)S(1)} %log_multiply_fusion), channel_id=1, source_target_pairs={{0,1},{1,0},{2,3},{3,2},{4,5},{5,4},{6,7},{7,6},{8,9},{9,8},{10,11... | collective-permute-start | bytes 98312 | tf_op jit(solution)/shard_map/ppermute | solution.py:276
  119.6 0.9 collective-permute-done.3
  120.5 0.7 copy.60
  (40 shorter events, 0.3 us)
Async XLA Ops:
  0.0 6.7 %copy-start = (bf16[2,8,1024]{2,1,0:T(8,128)(2,1)S(1)}, bf16[2,8,1024]{2,1,0:T(8,128)(2,1)}, u32[]{:S(2)}) copy-start(bf16[2,8,1024]{2,1,0:T(8,128)(2,1)} %param.7) | copy-start | bytes 98308
  0.8 24.7 %collective-permute-start = (f32[4]{0:T(128)S(1)}, f32[4]{0:T(128)S(1)}, u32[]{:S(2)}, u32[]{:S(2)}) collective-permute-start(f32[4]{0:T(128)S(1)} %pad_maximum_fusion.5), channel_id=1, source_target_pairs={{0,1},{1,0},{2,3},{3,2},{4,5},{5,4},{6,7},{7,6},{8,9},{9,8},{10,11... | collective-permute-start | bytes 56 | tf_op jit(solution)/shard_map/ppermute | solution.py:166
  7.6 28.6 %all-to-all-start = ((bf16[32,16,640]{2,1,0:T(8,128)(2,1)}), bf16[32,16,640]{2,1,0:T(8,128)(2,1)S(1)}, u32[]{:S(2)}, u32[]{:S(2)}) async-start(bf16[32,16,640]{2,1,0:T(8,128)(2,1)} %broadcast_in_dim.91), calls=%async_computation | async-start | bytes 1310720 | tf_op jit(solution)/shard_map/all_to_all | solution.py:43
  24.4 1.0 copy-start.6
  24.5 1.0 copy-start.7
  37.0 6.5 %copy-start.4 = (f32[16,12]{0,1:T(8,128)}, f32[16,12]{0,1:T(8,128)S(1)}, u32[]{:S(2)}) copy-start(f32[16,12]{0,1:T(8,128)S(1)} %select_reduce_fusion) | copy-start | bytes 2308
  38.6 28.8 %all-to-all-start.1 = ((bf16[4,32,16,512]{3,2,1,0:T(8,128)(2,1)}), bf16[4,32,16,512]{3,2,1,0:T(8,128)(2,1)}, u32[]{:S(2)}, u32[]{:S(2)}) async-start(bf16[4,32,16,512]{3,2,1,0:T(8,128)(2,1)} %broadcast_in_dim.104), calls=%async_computation.1 | async-start | bytes 4194304 | tf_op jit(solution)/shard_map/all_to_all | solution.py:43
  43.7 33.2 %slice-start = ((f32[16,12]{0,1:T(8,128)}), f32[16,2]{0,1:T(2,128)S(1)}, s32[]{:S(2)}) async-start(f32[16,12]{0,1:T(8,128)} %copy-done.4), calls=%async_computation.3 | async-start | bytes 2048 | tf_op jit(solution)/shard_map/slice | solution.py:194
  43.7 34.3 %copy-start.5 = (f32[16,12]{0,1:T(8,128)S(1)}, f32[16,12]{0,1:T(8,128)}, u32[]{:S(2)}) copy-start(f32[16,12]{0,1:T(8,128)} %copy-done.4) | copy-start | bytes 2308
  73.9 7.0 %collective-permute-start.1 = (bf16[32,128,256]{2,1,0:T(8,128)(2,1)}, bf16[32,128,256]{2,1,0:T(8,128)(2,1)S(1)}, u32[]{:S(2)}, u32[]{:S(2)}) collective-permute-start(bf16[32,128,256]{2,1,0:T(8,128)(2,1)} %bitcast.52), channel_id=1, source_target_pairs={{0,1},{1,0},{2,3},{3,2},{4,5},{5,4},{6,7},{7,6},{8,9},{9,8},{10,11... | collective-permute-start | bytes 6291464 | tf_op jit(solution)/shard_map/ppermute | solution.py:246
  80.8 1.6 %copy-start.1 = (bf16[8,4,128,256]{3,2,1,0:T(8,128)(2,1)S(1)}, bf16[8,4,128,256]{3,2,1,0:T(8,128)(2,1)}, u32[]{:S(2)}) copy-start(bf16[8,4,128,256]{3,2,1,0:T(8,128)(2,1)} %shard_map.73) | copy-start | bytes 6291460
  99.5 0.7 copy-start.2
  100.1 2.1 %collective-permute-start.2 = (f32[8,40,128]{2,1,0:T(8,128)S(1)}, f32[8,40,128]{2,1,0:T(8,128)S(1)}, u32[]{:S(2)}, u32[]{:S(2)}) collective-permute-start(f32[8,40,128]{2,1,0:T(8,128)S(1)} %get-tuple-element.8), channel_id=1, source_target_pairs={{0,1},{1,0},{2,3},{3,2},{4,5},{5,4},{6,7},{7,6},{8,9},{9,8},{10,11... | collective-permute-start | bytes 491528 | tf_op jit(solution)/shard_map/ppermute | solution.py:267
  102.3 0.7 copy-start.3
  117.2 3.2 %collective-permute-start.3 = (f32[2,32,128]{2,1,0:T(8,128)S(1)}, f32[2,32,128]{2,1,0:T(8,128)S(1)}, u32[]{:S(2)}, u32[]{:S(2)}) collective-permute-start(f32[2,32,128]{2,1,0:T(8,128)S(1)} %log_multiply_fusion), channel_id=1, source_target_pairs={{0,1},{1,0},{2,3},{3,2},{4,5},{5,4},{6,7},{7,6},{8,9},{9,8},{10,11... | collective-permute-start | bytes 98312 | tf_op jit(solution)/shard_map/ppermute | solution.py:276
where the time goes:
time: 122 us; the launch traced here: 121 us
  waiting for transfers between devices  35.7 us (29%)
  Pallas kernels  25.2 us (21%)
  starting transfers between devices  23.3 us (19%)
  blocking collectives  12.5 us (10%)
  other arithmetic  12.2 us (10%)
  local copies, waits for them, and re-layouts  8.03 us (7%)
  between operations  4.29 us (4%)
    all_to_all x2, waiting for transfers between devices, spread(): return lax.all_to_all(copies, axis, 0, 0)  32.7 us
    pallas_call x1, Pallas kernels, on_device(): pl.pallas_call(image_kernel, out_shape=[jax.ShapeDtypeStruct((8, PART_ROW...  17 us
    all_to_all x2, starting transfers between devices, spread(): return lax.all_to_all(copies, axis, 0, 0)  13.9 us
    all_to_all x1, blocking collectives, on_device(): terms = lax.all_to_all(terms, 'source', 0, 0, axis_index_groups=TILE_GROUPS)  12.5 us
    pallas_call x1, Pallas kernels, on_device(): pl.pallas_call(turn_kernel, grid=(8,), out_shape=jax.ShapeDtypeStruct((8,...  6.39 us
    convert_element_type x2, other arithmetic, phases(): return (jnp.cos(angle).astype(BF16), jnp.sin(angle).astype(BF16))  3.7 us
    ppermute x1, starting transfers between devices, on_device(): remote = lax.ppermute(local, 'cond', swap)  3.25 us
    ppermute x1, starting transfers between devices, on_device(): other = lax.ppermute(own, 'cond', swap)  2.99 us
  transfers between devices with their start and end apart: 6, of which 4 were waited for; matrix products, arithmetic and copies ran while one was open for 11% of the time, Pallas kernels for 0%

commit v1 on v0

v1 whole, which is shorter than its diff:
```python
import functools
import math

import jax
import jax.numpy as jnp
from jax import lax
from jax.experimental import pallas as pl
from jax.experimental.pallas import tpu as pltpu
from jax.sharding import PartitionSpec as P

N = 4096
BLOCK = 128
NB = 8
XR = 128
SPEC = 1024
SOURCES = 32
SLOTS = 8
CONDS = 4
W = 64
ROWS = 72
PART = 32
PART_ROWS = 40
GROUP = 16
LOCAL = SOURCES // 2
ENTRIES = LOCAL * SLOTS

TAU = 0.5
BACKGROUND = 0.05

MIB = 1024 * 1024
F32 = jnp.float32
BF16 = jnp.bfloat16

Z_GROUPS = [[z * 4 + y for z in range(8)] for y in range(4)]
PLANE_GROUPS = [[z * 16 + n for n in range(16)] for z in range(8)]
TILE_GROUPS = [[8 * k + t for k in range(4) for t in (q, 7 - q)] for q in range(4)]


def turn_by(angle, quarter):
    square = angle * angle
    sine = 1.0 + square * (-1.0 / 6.0 + square * (1.0 / 120.0 + square * (-1.0 / 5040.0 + square * (1.0 / 362880.0))))
    sine = angle * sine
    cosine = 1.0 + square * (-0.5 + square * (1.0 / 24.0 + square * (-1.0 / 720.0 + square * (1.0 / 40320.0))))
    odd = (quarter & 1) == 1
    first, second = jnp.where(odd, sine, cosine), jnp.where(odd, cosine, sine)
    cosine = jnp.where(((quarter + 1) & 2) == 2, -first, first)
    sine = jnp.where((quarter & 2) == 2, -second, second)
    return cosine, sine


def phases(product):
    turn = product & (N - 1)
    quarter = (turn + N // 8) >> 10
    return turn_by((turn - (quarter << 10)).astype(F32) * (2.0 * math.pi / N), quarter)


def pupil_factor(gap, focus):
    radius = gap * gap * (1.0 / (4.0 * BLOCK * BLOCK))
    amplitude = jnp.exp(-radius)
    angle = focus * radius
    quarter = jnp.floor(angle * (2.0 / math.pi) + 0.5)
    angle = angle - quarter * 1.5703125
    angle = angle - quarter * 4.837512969970703e-4
    angle = angle - quarter * 7.549789954891882e-8
    cosine, sine = turn_by(angle, quarter.astype(jnp.int32))
    return amplitude * cosine, amplitude * sine


def table_kernel(place_ref, rowf_ref, colf_ref):
    first_row, first_column = place_ref[0], place_ref[1]
    u = lax.broadcasted_iota(jnp.int32, (BLOCK, XR), 0) - SPEC // 2
    x = lax.broadcasted_iota(jnp.int32, (BLOCK, XR), 1) + first_row
    y = lax.broadcasted_iota(jnp.int32, (ROWS, BLOCK), 0) + first_column
    lane = lax.broadcasted_iota(jnp.int32, (ROWS, BLOCK), 1)
    v = (lane & 31) * 4 + (lane >> 5) - SPEC // 2

    def body(n, carry):
        cosine, sine = phases((u + n * BLOCK) * x)
        cosine, sine, minus = cosine.astype(BF16), sine.astype(BF16), (-sine).astype(BF16)
        rowf_ref[n, :BLOCK, :XR] = cosine
        rowf_ref[n, :BLOCK, XR:] = sine
        rowf_ref[n, BLOCK:, :XR] = minus
        rowf_ref[n, BLOCK:, XR:] = cosine
        both = jnp.concatenate(phases((v + n * BLOCK) * y), axis=0)
        colf_ref[n, 0] = both.astype(BF16)
        for d in (1, 2, 3):
            colf_ref[n, d] = pltpu.roll(both, 32 * d, 1).astype(BF16)
        return carry

    lax.fori_loop(0, NB, body, 0)
    colf_ref[NB] = jnp.zeros((4, 2 * ROWS, BLOCK), BF16)


def round_bf16(value):
    return value.astype(BF16).astype(F32)


def pack_kernel(core_ref, centers_ref, counts_ref, weights_ref, blocks_ref, spectrum_ref, out_ref):
    start = pl.multiple_of(512 * core_ref[0], 512)
    half = spectrum_ref[:, :, pl.ds(start, 512)].astype(F32).reshape(16, 512).astype(BF16)
    rows = lax.broadcasted_iota(jnp.int32, (BLOCK, BLOCK), 0)
    lanes = lax.broadcasted_iota(jnp.int32, (BLOCK, BLOCK), 1)
    select = (rows == (lanes & 31) * 4 + (lanes >> 5)).astype(F32).astype(BF16)
    parts = [
        jnp.dot(half[:, 128 * j:128 * j + 128], select, preferred_element_type=F32).astype(BF16)
        for j in range(4)
    ]
    numbers = [centers_ref[0, 0], centers_ref[0, 1], counts_ref[0, 0].astype(F32), weights_ref[0, 0]]
    numbers += [blocks_ref[0, k].astype(F32) for k in range(SLOTS)]
    lane = lax.broadcasted_iota(jnp.int32, (16, 128), 1)
    info = jnp.zeros((16, 128), F32)
    for n, value in enumerate(numbers):
        info = jnp.where(lane & 15 == n, value, info)
    high = round_bf16(info)
    mid = round_bf16(info - high)
    low = info - high - mid
    info = jnp.where(lane < 16, high, jnp.where(lane < 32, mid, low)).astype(BF16)
    for n in range(8):
        for j in range(4):
            out_ref[n, j] = parts[j]
        out_ref[n, 4] = info


def spread_kernel(column_ref, out_ref):
    row = lax.broadcasted_iota(jnp.int32, (16, 128), 0)
    info = jnp.zeros((16, 128), F32)
    for n in range(8):
        info = jnp.where(row == n, column_ref[n, 4].astype(F32)[0:1], info)
    info = info.astype(BF16)
    for m in range(16):
        for n in range(8):
            out_ref[m, 4 * n:4 * n + 4] = column_ref[n, :4]
        out_ref[m, 32] = info


def turn_kernel(rows_ref, out_ref):
    for i in range(2):
        for j in range(4):
            parts = [rows_ref[n, 4 * i + j].astype(F32) for n in range(16)]
            stack = jnp.concatenate([p[:8] for p in parts] + [p[8:] for p in parts], axis=0)
            out_ref[i, j] = jnp.transpose(stack.astype(BF16))


def image_kernel(
    info_ref, whole_ref, focus_ref, core_ref, own_ref, other_ref, rowf_ref, colf_ref,
    keep_ref, send_ref, turned, pieces, power, even, odd, numbers, p_re, p_im, q_re, q_im, listing, sems,
):
    def count_of(s):
        return whole_ref[16 * s + 2]

    def block_of(e):
        return whole_ref[((e >> 3) << 4) + 4 + (e & 7)]

    copies = [
        pltpu.make_async_copy(ref, turned.at[pl.ds(32 * n, 32)], sems.at[n])
        for n, ref in enumerate((own_ref, other_ref))
    ]
    for copy in copies:
        copy.start()

    def live(s, total):
        for k in range(SLOTS):
            listing[total + k] = s * SLOTS + k
        return total + count_of(s)

    total = lax.fori_loop(0, LOCAL, live, 0)
    for n in range(GROUP):
        listing[total + n] = ENTRIES
    groups = (total + GROUP - 1) >> 4
    lane = lax.broadcasted_iota(jnp.int32, (SLOTS, BLOCK), 1)
    by_residue = ((lane & 31) * 4 + (lane >> 5)).astype(F32)
    lane = lane.astype(F32)
    for s in range(LOCAL):
        rows = slice(SLOTS * s, SLOTS * s + SLOTS)
        for k in range(SLOTS):
            numbers[SLOTS * s + k:SLOTS * s + k + 1, :] = jnp.full((1, BLOCK), info_ref[16 * s + 4 + k])
        number = numbers[rows, :]
        i = jnp.floor(number * (1.0 / NB))
        j = number - i * NB
        p_re[rows, :], p_im[rows, :] = pupil_factor(i * BLOCK + lane - info_ref[16 * s], focus_ref[0])
        q_re[rows, :], q_im[rows, :] = pupil_factor(j * BLOCK + by_residue - info_ref[16 * s + 1], focus_ref[0])

    pieces[...] = jnp.zeros_like(pieces)
    power[...] = jnp.zeros_like(power)
    for copy in copies:
        copy.wait()

    def entries(g, carry):
        places = [listing[g * GROUP + n] for n in range(GROUP)]
        sources = [jnp.minimum(e, ENTRIES - 1) for e in places]
        q_all = jnp.transpose(
            jnp.concatenate([part[pl.ds(e, 1), :] for part in (q_re, q_im) for e in sources], axis=0)
        )
        for n in range(GROUP):
            number = block_of(sources[n])
            i, j = number >> 3, number & 7
            block = turned[(((j >> 2) ^ core_ref[0]) << 5) + (i << 2) + (j & 3)].astype(F32)
            re, im = block[:, :128], block[:, 128:]
            pr, pi = p_re[pl.ds(sources[n], 1), :], p_im[pl.ds(sources[n], 1), :]
            qr, qi = q_all[:, n:n + 1], q_all[:, GROUP + n:GROUP + n + 1]
            pupil_re = qr * pr - qi * pi
            pupil_im = qr * pi + qi * pr
            masked_re = (re * pupil_re - im * pupil_im).astype(BF16)
            masked_im = (re * pupil_im + im * pupil_re).astype(BF16)
            masked = jnp.concatenate([masked_re, masked_im], axis=1)
            piece = jnp.dot(masked, rowf_ref[i], preferred_element_type=F32).astype(BF16)
            place = pl.ds(pl.multiple_of(32 * (places[n] & 7), 32), 32)
            for r in range(4):
                pieces[places[n] >> 3, r, place, :] = piece[32 * r:32 * r + 32]
        return carry

    lax.fori_loop(0, groups, entries, 0)

    lane_group = lax.broadcasted_iota(jnp.int32, (2 * ROWS, 128), 1) // 32

    def transform(s, buffer):
        columns = [
            jnp.where(k < count_of(s), whole_ref[16 * s + 4 + k] & 7, NB) for k in range(SLOTS)
        ]
        for r in range(4):
            halves = []
            for h in range(2):
                table = None
                for m in range(4):
                    term = colf_ref[columns[4 * h + m], (m - r) % 4]
                    table = term if table is None else jnp.where(lane_group == m, term, table)
                halves.append(table)
            table = jnp.concatenate(halves, axis=1)
            buffer[r] = jnp.dot(table, pieces[s, r], preferred_element_type=F32)

    def gather_power(s, buffer):
        weight = info_ref[16 * s + 3]
        for c in range(ROWS // 8):
            low = slice(8 * c, 8 * c + 8)
            high = slice(ROWS + 8 * c, ROWS + 8 * c + 8)
            direct, mirror = [], []
            for r in range(4):
                a_cos, b_cos = buffer[r, low, :128], buffer[r, low, 128:]
                a_sin, b_sin = buffer[r, high, :128], buffer[r, high, 128:]
                direct.append((a_cos - b_sin, a_sin + b_cos))
                mirror.append((a_cos + b_sin, b_cos - a_sin))
            for base, parts in ((0, direct), (4, mirror)):
                (r0, i0), (r1, i1), (r2, i2), (r3, i3) = parts
                gr, gi, dr, di = r0 + r2, i0 + i2, r0 - r2, i0 - i2
                hr, hi, er, ei = r1 + r3, i1 + i3, r1 - r3, i1 - i3
                images = ((gr + hr, gi + hi), (dr - ei, di + er), (gr - hr, gi - hi), (dr + ei, di - er))
                for m, (fr, fi) in enumerate(images):
                    power[base + m, low] += weight * (fr * fr + fi * fi)

    transform(0, even)
    def two(i, carry):
        gather_power(2 * i, even)
        transform(2 * i + 1, odd)
        gather_power(2 * i + 1, odd)
        transform(jnp.minimum(2 * i + 2, LOCAL - 1), even)
        return carry
    lax.fori_loop(0, LOCAL // 2, two, 0)
    mine = pl.multiple_of(PART * core_ref[0], PART)
    theirs = pl.multiple_of(PART * (1 - core_ref[0]), PART)
    for image in range(8):
        keep_ref[image] = power[image, pl.ds(mine, PART_ROWS), :]
        send_ref[image] = power[image, pl.ds(theirs, PART_ROWS), :]


def slope_kernel(dose_ref, keep_ref, other_ref, out_ref):
    dose = dose_ref[0]
    for e in range(8):
        image = e // 2 if e % 2 == 0 else 4 + (e // 2 + 1) % 4
        low = 1 + e % 2
        level = dose * (keep_ref[image] + other_ref[image]) / SOURCES + BACKGROUND
        slope = jnp.abs(level[low + 1:low + 1 + PART] - level[low - 1:low - 1 + PART]) / (
            2.0 * level[low:low + PART]
        )
        out_ref[e] = jnp.exp(slope * (-1.0 / TAU))


def on_device(spectrum, centers, blocks, counts, weights, defocus, dose_scale):
    core = lax.axis_index("cond")
    source = lax.axis_index("source")
    z, y = source // 4, source % 4
    swap = [(0, 1), (1, 0)]
    vmem = pl.BlockSpec(memory_space=pltpu.VMEM)
    smem = pl.BlockSpec(memory_space=pltpu.SMEM)
    hbm = pl.BlockSpec(memory_space=pl.ANY)
    packed = pl.pallas_call(
        pack_kernel,
        out_shape=jax.ShapeDtypeStruct((8, 5, 16, 128), BF16),
        in_specs=[smem] * 5 + [vmem],
        out_specs=vmem,
        compiler_params=pltpu.CompilerParams(vmem_limit_bytes=56 * MIB),
    )(core.reshape(1), centers, counts.reshape(1, 1), weights.reshape(1, 1), blocks, spectrum)
    defocus, dose_scale, packed = lax.optimization_barrier((defocus, dose_scale, packed))

    local = jnp.concatenate([defocus, dose_scale])
    remote = lax.ppermute(local, "cond", swap)
    cond = z % 4
    chosen = jnp.where(cond // 2 == core, local, remote)
    focus = jnp.where(cond % 2 == 0, chosen[0], chosen[1])
    dose = jnp.where(cond % 2 == 0, chosen[2], chosen[3])
    quarter = jnp.where(z % 2 == 0, y, 3 - y)
    window = 2 * quarter + z // 4
    place = jnp.stack([lax.axis_index("row") * XR, window * W - 1])
    place, packed = lax.optimization_barrier((place, packed))
    rowf, colf = pl.pallas_call(
        table_kernel,
        out_shape=[
            jax.ShapeDtypeStruct((NB, 2 * BLOCK, 2 * XR), BF16),
            jax.ShapeDtypeStruct((NB + 1, 4, 2 * ROWS, BLOCK), BF16),
        ],
        in_specs=[smem],
        out_specs=[vmem, vmem],
        compiler_params=pltpu.CompilerParams(vmem_limit_bytes=8 * MIB),
    )(place)

    column = lax.all_to_all(packed, "source", 0, 0, axis_index_groups=Z_GROUPS)
    copies = pl.pallas_call(
        spread_kernel,
        out_shape=jax.ShapeDtypeStruct((16, 33, 16, 128), BF16),
        in_specs=[vmem],
        out_specs=vmem,
        compiler_params=pltpu.CompilerParams(vmem_limit_bytes=4 * MIB),
    )(column)
    rows = lax.all_to_all(copies, ("source", "row"), 0, 0, axis_index_groups=PLANE_GROUPS)
    rows, rowf, colf, dose, focus = lax.optimization_barrier((rows, rowf, colf, dose, focus))
    own = pl.pallas_call(
        turn_kernel,
        grid=(4,),
        out_shape=jax.ShapeDtypeStruct((8, 4, 128, 256), BF16),
        in_specs=[pl.BlockSpec((16, 8, 16, 128), lambda i: (0, i, 0, 0))],
        out_specs=pl.BlockSpec((2, 4, 128, 256), lambda i: (i, 0, 0, 0)),
        compiler_params=pltpu.CompilerParams(vmem_limit_bytes=8 * MIB),
    )(rows)
    own = own.reshape(32, 128, 256)
    other = lax.ppermute(own, "cond", swap)

    info = lax.dynamic_slice(rows, (8 * core, 32, 0, 0), (8, 1, 8, 48))[::4, 0].astype(F32)
    info = (info[:, :, :16] + info[:, :, 16:32] + info[:, :, 32:]).reshape(-1)
    keep, send = pl.pallas_call(
        image_kernel,
        out_shape=[jax.ShapeDtypeStruct((8, PART_ROWS, XR), F32)] * 2,
        in_specs=[smem] * 4 + [hbm] * 2 + [vmem] * 2,
        out_specs=[vmem] * 2,
        scratch_shapes=[
            pltpu.VMEM((64, 128, 256), BF16),
            pltpu.VMEM((LOCAL + 1, 4, 256, 256), BF16),
            pltpu.VMEM((8, ROWS, XR), F32),
            pltpu.VMEM((4, 2 * ROWS, 256), F32),
            pltpu.VMEM((4, 2 * ROWS, 256), F32),
        ] + [pltpu.VMEM((ENTRIES, BLOCK), F32)] * 5 + [
            pltpu.SMEM((ENTRIES + GROUP,), jnp.int32),
            pltpu.SemaphoreType.DMA((2,)),
        ],
        compiler_params=pltpu.CompilerParams(vmem_limit_bytes=24 * MIB),
    )(info, info.astype(jnp.int32), focus.reshape(1), core.reshape(1), own, other, rowf, colf)
    received = lax.ppermute(send, "cond", swap)
    terms = pl.pallas_call(
        slope_kernel,
        out_shape=jax.ShapeDtypeStruct((8, PART, XR), F32),
        in_specs=[smem, vmem, vmem],
        out_specs=vmem,
        compiler_params=pltpu.CompilerParams(vmem_limit_bytes=4 * MIB),
    )(dose.reshape(1), keep, received)
    terms = lax.all_to_all(terms, "source", 0, 0, axis_index_groups=TILE_GROUPS)
    soft = -TAU * jnp.log(jnp.sum(terms.reshape(2, CONDS, PART, XR), axis=1) / CONDS)
    theirs = lax.ppermute(soft, "cond", swap)
    first, second = jnp.where(core == 0, soft, theirs), jnp.where(core == 0, theirs, soft)
    soft = jnp.stack([first, second], axis=1).reshape(2 * W, XR)
    soft = jnp.where(z % 2 == 0, soft, soft[::-1])
    return soft.T


def solution(mesh):
    in_specs = (
        P(None, ("source", "row"), None),
        P("source", None),
        P("source", None),
        P("source"),
        P("source"),
        P("cond"),
        P("cond"),
    )
    out_specs = P("row", "source")
    return jax.shard_map(
        on_device, mesh=mesh, in_specs=in_specs, out_specs=out_specs, check_vma=False
    )
```

time: 122 us -> 98.5 us (0.81)
  blocking collectives: 12.5 us -> 28.2 us
  waiting for transfers between devices: 35.7 us -> 22 us
  other arithmetic: 12.2 us -> 0.37 us
  Pallas kernels: 25.2 us -> 18.8 us
  starting transfers between devices: 23.3 us -> 19.8 us
  local copies, waits for them, and re-layouts: 8.03 us -> 5.02 us
    all_to_all x0 -> x1, blocking collectives: none -> 17.2 us  [on_device(): column = lax.all_to_all(packed, 'source', 0, 0, axis_index_groups=Z_GROUPS)]
    all_to_all x2 -> x1, waiting for transfers between devices: 32.7 us -> 16.2 us  [on_device(): lax.all_to_all(copies, ('source', 'row'), 0, 0, axis_index_groups=PLANE_G...]
    all_to_all x2 -> x1, starting transfers between devices: 13.9 us -> 6.89 us  [on_device(): lax.all_to_all(copies, ('source', 'row'), 0, 0, axis_index_groups=PLANE_G...]
    pallas_call x1, Pallas kernels: 17 us -> 11.6 us  [on_device(): pl.pallas_call(image_kernel, out_shape=[jax.ShapeDtypeStruct((8, PART_ROW...]
    convert_element_type x6 -> x2, other arithmetic: 5.07 us -> 0.01 us  [the longest x1 0.01 us: on_device(): info.astype(jnp.int32)]
    ppermute x1, starting transfers between devices: 2.99 us -> 5.95 us  [on_device(): other = lax.ppermute(own, 'cond', swap)]
    broadcast_in_dim x2 -> x0, local copies, waits for them, and re-layouts: 2.47 us -> none  [spread(): copies = jnp.broadcast_to(value[None], (count,) + value.shape)]
    neg x1 -> x0, other arithmetic: 2.14 us -> none  [on_device(): -row_sin]
  transfers between devices with their start and end apart: 6 -> 5, of which waited for: 4 -> 4; matrix products, arithmetic and copies ran while one was open for 11% -> 1% of each run, Pallas kernels for 0% -> 3%
where the time goes in v1:
time: 98.5 us; the launch traced here: 98.1 us
  blocking collectives  28.2 us (29%)
  waiting for transfers between devices  22 us (22%)
  starting transfers between devices  19.8 us (20%)
  Pallas kernels  18.8 us (19%)
  local copies, waits for them, and re-layouts  5.02 us (5%)
  between operations  3.96 us (4%)
    all_to_all x1, blocking collectives, on_device(): column = lax.all_to_all(packed, 'source', 0, 0, axis_index_groups=Z_GROUPS)  17.2 us
    all_to_all x1, waiting for transfers between devices, on_device(): lax.all_to_all(copies, ('source', 'row'), 0, 0, axis_index_groups=PLANE_G...  16.2 us
    pallas_call x1, Pallas kernels, on_device(): pl.pallas_call(image_kernel, out_shape=[jax.ShapeDtypeStruct((8, PART_ROW...  11.6 us
    all_to_all x1, blocking collectives, on_device(): terms = lax.all_to_all(terms, 'source', 0, 0, axis_index_groups=TILE_GROUPS)  11.1 us
    all_to_all x1, starting transfers between devices, on_device(): lax.all_to_all(copies, ('source', 'row'), 0, 0, axis_index_groups=PLANE_G...  6.89 us
    ppermute x1, starting transfers between devices, on_device(): other = lax.ppermute(own, 'cond', swap)  5.95 us
    ppermute x1, waiting for transfers between devices, on_device(): other = lax.ppermute(own, 'cond', swap)  3.95 us
    unnamed x10, local copies, waits for them, and re-layouts  3.53 us
  transfers between devices with their start and end apart: 5, of which 4 were waited for; matrix products, arithmetic and copies ran while one was open for 1% of the time, Pallas kernels for 3%

profile of v1, /device:TPU:1, one launch (start us, length us, event | category | flops | bytes accessed | tf_op | source)
XLA Modules:
  0.0 98.1 jit_solution(14982702111814133411)
XLA Ops:
  1.3 1.6 %shard_map.73 = bf16[8,5,16,128]{3,2,1,0:T(8,128)(2,1)} custom-call(s32[1]{0:T(128)} %bitcast.2.core_ref, f32[1,2]{1,0:T(1,128)} %centers_ref.1, s32[1,1]{1,0:T(1,128)} %bitcast.27.counts_ref, f32[1,1]{1,0:T(1,128)} %bitcast.28.weights_ref, s32[1,8]{1,0:T(1,128)} %blocks_ref.1, bf16[2,8,1024]{2,1,0:T(8,128)(2,1)} %spectrum_ref.1), custom_call_target="tpu_custom_call" | custom-call | tf_op jit(solution)/shard_map/pallas_call | solution.py:285
  2.9 0.1 pad_add_fusion.place_ref
  3.0 17.2 %all_to_all.15.column_ref = bf16[8,5,16,128]{3,2,1,0:T(8,128)(2,1)S(1)} all-to-all(bf16[8,5,16,128]{3,2,1,0:T(8,128)(2,1)} %shard_map.73), channel_id=1, replica_groups={{0,32,64,96,128,160,192,224},{8,40,72,104,136,168,200,232},{16,48,80,11..., dimensions={0} | all-to-all | bytes 327680 | tf_op jit(solution)/shard_map/all_to_all | solution.py:315
  20.1 0.3 shard_map.74
  20.4 0.0 copy-start
  20.4 1.3 %copy-done = bf16[16,33,16,128]{3,2,1,0:T(8,128)(2,1)} copy-done((bf16[16,33,16,128]{3,2,1,0:T(8,128)(2,1)}, bf16[16,33,16,128]{3,2,1,0:T(8,128)(2,1)S(1)}, u32[]{:S(2)}) %copy-start) | copy-done | bytes 2162712
  21.8 0.0 copy-start.3
  21.8 0.0 copy-start.4
  21.8 6.9 %all-to-all-start.1 = ((bf16[16,33,16,128]{3,2,1,0:T(8,128)(2,1)}), bf16[16,33,16,128]{3,2,1,0:T(8,128)(2,1)S(1)}, u32[]{:S(2)}, u32[]{:S(2)}) async-start(bf16[16,33,16,128]{3,2,1,0:T(8,128)(2,1)} %copy-done), calls=%async_computation.1 | async-start | bytes 4325376 | tf_op jit(solution)/shard_map/all_to_all | solution.py:323
  28.7 0.0 copy-done.3
  28.7 0.0 copy-done.4
  28.7 0.1 pad_maximum_fusion.1
  28.8 2.9 %collective-permute-start = (f32[4]{0:T(128)S(1)}, f32[4]{0:T(128)S(1)}, u32[]{:S(2)}, u32[]{:S(2)}) collective-permute-start(f32[4]{0:T(128)S(1)} %pad_maximum_fusion.1), channel_id=1, source_target_pairs={{0,1},{1,0},{2,3},{3,2},{4,5},{5,4},{6,7},{7,6},{8,9},{9,8},{10,11... | collective-permute-start | bytes 56 | tf_op jit(solution)/shard_map/ppermute | solution.py:295
  31.6 2.6 %shard_map.75 = (bf16[8,256,256]{2,1,0:T(8,128)(2,1)S(1)}, bf16[9,4,144,128]{3,2,1,0:T(8,128)(2,1)S(1)}) custom-call(s32[2]{0:T(128)S(1)} %pad_add_fusion.place_ref), custom_call_target="tpu_custom_call" | custom-call | tf_op jit(solution)/shard_map/pallas_call | solution.py:304
  34.2 0.0 copy-start.1
  34.3 1.0 copy-done.1
  35.2 0.0 collective-permute-done
  35.2 0.1 broadcast_select_fusion
  35.3 0.7 fusion
  38.5 16.2 %all-to-all-done.1.rows_ref = bf16[16,33,16,128]{3,2,1,0:T(8,128)(2,1)S(1)} async-done(((bf16[16,33,16,128]{3,2,1,0:T(8,128)(2,1)}), bf16[16,33,16,128]{3,2,1,0:T(8,128)(2,1)S(1)}, u32[]{:S(2)}, u32[]{:S(2)}) %all-to-all-start.1) | async-done | bytes 2162720 | tf_op jit(solution)/shard_map/all_to_all | solution.py:323
  54.7 2.6 %shard_map.76 = bf16[8,4,128,256]{3,2,1,0:T(8,128)(2,1)} custom-call(bf16[16,33,16,128]{3,2,1,0:T(8,128)(2,1)S(1)} %all-to-all-done.1.rows_ref), custom_call_target="tpu_custom_call" | custom-call | tf_op jit(solution)/shard_map/pallas_call | solution.py:325
  57.2 6.0 %collective-permute-start.1 = (bf16[32,128,256]{2,1,0:T(8,128)(2,1)}, bf16[32,128,256]{2,1,0:T(8,128)(2,1)}, u32[]{:S(2)}, u32[]{:S(2)}) collective-permute-start(bf16[32,128,256]{2,1,0:T(8,128)(2,1)} %bitcast.13.own_ref), channel_id=1, source_target_pairs={{0,1},{1,0},{2,3},{3,2},{4,5},{5,4},{6,7},{7,6},{8,9},{9,8},{10,11... | collective-permute-start | bytes 6291464 | tf_op jit(solution)/shard_map/ppermute | solution.py:334
  63.2 0.1 slice_add_fusion
  63.3 0.1 reshape.34.info_ref
  63.4 4.0 %collective-permute-done.1.other_ref = bf16[32,128,256]{2,1,0:T(8,128)(2,1)} collective-permute-done((bf16[32,128,256]{2,1,0:T(8,128)(2,1)}, bf16[32,128,256]{2,1,0:T(8,128)(2,1)}, u32[]{:S(2)}, u32[]{:S(2)}) %collective-permute-start.1) | collective-permute-done | bytes 2097184 | tf_op jit(solution)/shard_map/ppermute | solution.py:334
  67.3 0.0 copy-start.2
  67.3 1.2 %copy-done.2 = bf16[8,256,256]{2,1,0:T(8,128)(2,1)S(1)} copy-done((bf16[8,256,256]{2,1,0:T(8,128)(2,1)S(1)}, bf16[8,256,256]{2,1,0:T(8,128)(2,1)}, u32[]{:S(2)}) %copy-start.2) | copy-done | bytes 1048600
  68.5 11.6 %shard_map.77 = (f32[8,40,128]{2,1,0:T(8,128)S(1)}, f32[8,40,128]{2,1,0:T(8,128)S(1)}) custom-call(f32[256]{0:T(256)S(1)} %reshape.34.info_ref, s32[256]{0:T(256)S(1)} %convert_element_type.11.whole_ref, f32[1]{0:T(128)} %bitcast.12.focus_ref, s32[1]{0:T(128)} %bitcast.2.core_ref, bf16[32,128,256]{2,1,0:T(8,128)(2,1)} %bitcast.13.own_ref, ...), custom_call_target="tpu_custom_call" | custom-call | tf_op jit(solution)/shard_map/pallas_call | solution.py:338
  80.2 1.6 %collective-permute-start.2 = (f32[8,40,128]{2,1,0:T(8,128)S(1)}, f32[8,40,128]{2,1,0:T(8,128)S(1)}, u32[]{:S(2)}, u32[]{:S(2)}) collective-permute-start(f32[8,40,128]{2,1,0:T(8,128)S(1)} %get-tuple-element.32), channel_id=1, source_target_pairs={{0,1},{1,0},{2,3},{3,2},{4,5},{5,4},{6,7},{7,6},{8,9},{9,8},{10,11... | collective-permute-start | bytes 491528 | tf_op jit(solution)/shard_map/ppermute | solution.py:355
  81.7 1.0 %collective-permute-done.2.other_ref = f32[8,40,128]{2,1,0:T(8,128)S(1)} collective-permute-done((f32[8,40,128]{2,1,0:T(8,128)S(1)}, f32[8,40,128]{2,1,0:T(8,128)S(1)}, u32[]{:S(2)}, u32[]{:S(2)}) %collective-permute-start.2) | collective-permute-done | bytes 163872 | tf_op jit(solution)/shard_map/ppermute | solution.py:355
  82.8 0.1 shard_map.78
  82.9 11.1 %all_to_all.16 = f32[8,32,128]{2,1,0:T(8,128)S(1)} all-to-all(f32[8,32,128]{2,1,0:T(8,128)S(1)} %shard_map.78), channel_id=1, replica_groups={{0,56,64,120,128,184,192,248},{8,48,72,112,136,176,200,240},{16,40,80,1..., dimensions={0} | all-to-all | bytes 262144 | tf_op jit(solution)/shard_map/all_to_all | solution.py:363
  94.0 2.5 %collective-permute-start.3 = (f32[2,32,128]{2,1,0:T(8,128)S(1)}, f32[2,32,128]{2,1,0:T(8,128)S(1)}, u32[]{:S(2)}, u32[]{:S(2)}) collective-permute-start(f32[2,32,128]{2,1,0:T(8,128)S(1)} %log_multiply_fusion), channel_id=1, source_target_pairs={{0,1},{1,0},{2,3},{3,2},{4,5},{5,4},{6,7},{7,6},{8,9},{9,8},{10,11... | collective-permute-start | bytes 98312 | tf_op jit(solution)/shard_map/ppermute | solution.py:365
  96.5 0.9 collective-permute-done.3
  97.4 0.7 copy.10
  (9 shorter events, 0.1 us)
Async XLA Ops:
  20.4 1.4 %copy-start = (bf16[16,33,16,128]{3,2,1,0:T(8,128)(2,1)}, bf16[16,33,16,128]{3,2,1,0:T(8,128)(2,1)S(1)}, u32[]{:S(2)}) copy-start(bf16[16,33,16,128]{3,2,1,0:T(8,128)(2,1)S(1)} %shard_map.74) | copy-start | bytes 6488068
  21.8 6.9 %copy-start.3 = (f32[2]{0:T(128)S(1)}, f32[2]{0:T(128)}, u32[]{:S(2)}) copy-start(f32[2]{0:T(128)} %param.13) | copy-start | bytes 28
  21.8 6.9 %copy-start.4 = (f32[2]{0:T(128)S(1)}, f32[2]{0:T(128)}, u32[]{:S(2)}) copy-start(f32[2]{0:T(128)} %param.12) | copy-start | bytes 28
  21.8 32.9 %all-to-all-start.1 = ((bf16[16,33,16,128]{3,2,1,0:T(8,128)(2,1)}), bf16[16,33,16,128]{3,2,1,0:T(8,128)(2,1)S(1)}, u32[]{:S(2)}, u32[]{:S(2)}) async-start(bf16[16,33,16,128]{3,2,1,0:T(8,128)(2,1)} %copy-done), calls=%async_computation.1 | async-start | bytes 4325376 | tf_op jit(solution)/shard_map/all_to_all | solution.py:323
  28.8 6.5 %collective-permute-start = (f32[4]{0:T(128)S(1)}, f32[4]{0:T(128)S(1)}, u32[]{:S(2)}, u32[]{:S(2)}) collective-permute-start(f32[4]{0:T(128)S(1)} %pad_maximum_fusion.1), channel_id=1, source_target_pairs={{0,1},{1,0},{2,3},{3,2},{4,5},{5,4},{6,7},{7,6},{8,9},{9,8},{10,11... | collective-permute-start | bytes 56 | tf_op jit(solution)/shard_map/ppermute | solution.py:295
  34.2 1.0 copy-start.1
  57.2 10.1 %collective-permute-start.1 = (bf16[32,128,256]{2,1,0:T(8,128)(2,1)}, bf16[32,128,256]{2,1,0:T(8,128)(2,1)}, u32[]{:S(2)}, u32[]{:S(2)}) collective-permute-start(bf16[32,128,256]{2,1,0:T(8,128)(2,1)} %bitcast.13.own_ref), channel_id=1, source_target_pairs={{0,1},{1,0},{2,3},{3,2},{4,5},{5,4},{6,7},{7,6},{8,9},{9,8},{10,11... | collective-permute-start | bytes 6291464 | tf_op jit(solution)/shard_map/ppermute | solution.py:334
  67.3 1.2 %copy-start.2 = (bf16[8,256,256]{2,1,0:T(8,128)(2,1)S(1)}, bf16[8,256,256]{2,1,0:T(8,128)(2,1)}, u32[]{:S(2)}) copy-start(bf16[8,256,256]{2,1,0:T(8,128)(2,1)} %copy-done.1) | copy-start | bytes 3145732
  80.2 2.6 %collective-permute-start.2 = (f32[8,40,128]{2,1,0:T(8,128)S(1)}, f32[8,40,128]{2,1,0:T(8,128)S(1)}, u32[]{:S(2)}, u32[]{:S(2)}) collective-permute-start(f32[8,40,128]{2,1,0:T(8,128)S(1)} %get-tuple-element.32), channel_id=1, source_target_pairs={{0,1},{1,0},{2,3},{3,2},{4,5},{5,4},{6,7},{7,6},{8,9},{9,8},{10,11... | collective-permute-start | bytes 491528 | tf_op jit(solution)/shard_map/ppermute | solution.py:355
  94.0 3.4 %collective-permute-start.3 = (f32[2,32,128]{2,1,0:T(8,128)S(1)}, f32[2,32,128]{2,1,0:T(8,128)S(1)}, u32[]{:S(2)}, u32[]{:S(2)}) collective-permute-start(f32[2,32,128]{2,1,0:T(8,128)S(1)} %log_multiply_fusion), channel_id=1, source_target_pairs={{0,1},{1,0},{2,3},{3,2},{4,5},{5,4},{6,7},{7,6},{8,9},{9,8},{10,11... | collective-permute-start | bytes 98312 | tf_op jit(solution)/shard_map/ppermute | solution.py:365

commit v2 on v1

--- a/solution.py
+++ b/solution.py
@@ -32,7 +32,8 @@
 BF16 = jnp.bfloat16
 
 Z_GROUPS = [[z * 4 + y for z in range(8)] for y in range(4)]
-PLANE_GROUPS = [[z * 16 + n for n in range(16)] for z in range(8)]
+X_LINES = [[[((z * 4 + y) * 4 + x) * 2 + c for x in range(4)] for z in range(8) for y in range(4)] for c in range(2)]
+Y_LINES = [[[((z * 4 + y) * 4 + x) * 2 + c for y in range(4)] for z in range(8) for x in range(4)] for c in range(2)]
 TILE_GROUPS = [[8 * k + t for k in range(4) for t in (q, 7 - q)] for q in range(4)]
 
 
@@ -127,23 +128,28 @@
     for n in range(8):
         info = jnp.where(row == n, column_ref[n, 4].astype(F32)[0:1], info)
     info = info.astype(BF16)
-    for m in range(16):
+    for m in range(4):
         for n in range(8):
             out_ref[m, 4 * n:4 * n + 4] = column_ref[n, :4]
         out_ref[m, 32] = info
 
 
-def turn_kernel(rows_ref, out_ref):
-    for i in range(2):
-        for j in range(4):
-            parts = [rows_ref[n, 4 * i + j].astype(F32) for n in range(16)]
-            stack = jnp.concatenate([p[:8] for p in parts] + [p[8:] for p in parts], axis=0)
-            out_ref[i, j] = jnp.transpose(stack.astype(BF16))
+def turned_block(rows_ref, at, carrier):
+    parts = [
+        rows_ref[jnp.where(carrier == 1, 4 * (n % 4) + n // 4, n), at].astype(F32) for n in range(16)
+    ]
+    stack = jnp.concatenate([p[:8] for p in parts] + [p[8:] for p in parts], axis=0)
+    return jnp.transpose(stack.astype(BF16))
+
+
+def turn_kernel(core_ref, rows_ref, out_ref):
+    for n in range(8):
+        out_ref[n] = turned_block(rows_ref, n, core_ref[0])
 
 
 def image_kernel(
-    info_ref, whole_ref, focus_ref, core_ref, own_ref, other_ref, rowf_ref, colf_ref,
-    keep_ref, send_ref, turned, pieces, power, even, odd, numbers, p_re, p_im, q_re, q_im, listing, sems,
+    info_ref, whole_ref, focus_ref, core_ref, own_ref, other_ref, rows_ref, columns_ref,
+    keep_ref, send_ref, raw, turned, rowf_ref, colf_ref, pieces, power, even, odd, numbers, p_re, p_im, q_re, q_im, listing, sems,
 ):
     def count_of(s):
         return whole_ref[16 * s + 2]
@@ -152,10 +158,17 @@
         return whole_ref[((e >> 3) << 4) + 4 + (e & 7)]
 
     copies = [
-        pltpu.make_async_copy(ref, turned.at[pl.ds(32 * n, 32)], sems.at[n])
-        for n, ref in enumerate((own_ref, other_ref))
+        pltpu.make_async_copy(ref, place, sems.at[n])
+        for n, (ref, place) in enumerate(
+            (
+                (other_ref, raw),
+                (own_ref, turned.at[pl.ds(0, 32)]),
+                (rows_ref, rowf_ref),
+                (columns_ref, colf_ref),
+            )
+        )
     ]
-    for copy in copies:
+    for copy in copies[:3]:
         copy.start()
 
     def live(s, total):
@@ -182,8 +195,17 @@
 
     pieces[...] = jnp.zeros_like(pieces)
     power[...] = jnp.zeros_like(power)
-    for copy in copies:
-        copy.wait()
+    copies[0].wait()
+    copies[3].start()
+
+    def turn(n, carry):
+        for m in range(8):
+            turned[32 + 8 * n + m] = turned_block(raw, 8 * n + m, 1 - core_ref[0])
+        return carry
+
+    lax.fori_loop(0, 4, turn, 0)
+    copies[1].wait()
+    copies[2].wait()
 
     def entries(g, carry):
         places = [listing[g * GROUP + n] for n in range(GROUP)]
@@ -210,6 +232,7 @@
         return carry
 
     lax.fori_loop(0, groups, entries, 0)
+    copies[3].wait()
 
     lane_group = lax.broadcasted_iota(jnp.int32, (2 * ROWS, 128), 1) // 32
 
@@ -289,7 +312,17 @@
         out_specs=vmem,
         compiler_params=pltpu.CompilerParams(vmem_limit_bytes=56 * MIB),
     )(core.reshape(1), centers, counts.reshape(1, 1), weights.reshape(1, 1), blocks, spectrum)
-    defocus, dose_scale, packed = lax.optimization_barrier((defocus, dose_scale, packed))
+    column = lax.all_to_all(packed, "source", 0, 0, axis_index_groups=Z_GROUPS)
+    copies = pl.pallas_call(
+        spread_kernel,
+        out_shape=jax.ShapeDtypeStruct((4, 33, 16, 128), BF16),
+        in_specs=[vmem],
+        out_specs=vmem,
+        compiler_params=pltpu.CompilerParams(vmem_limit_bytes=4 * MIB),
+    )(column)
+    every = ("source", "row", "cond")
+    line = lax.all_to_all(copies, every, 0, 0, axis_index_groups=X_LINES[0] + Y_LINES[1])
+    defocus, dose_scale, line = lax.optimization_barrier((defocus, dose_scale, line))
 
     local = jnp.concatenate([defocus, dose_scale])
     remote = lax.ppermute(local, "cond", swap)
@@ -300,7 +333,7 @@
     quarter = jnp.where(z % 2 == 0, y, 3 - y)
     window = 2 * quarter + z // 4
     place = jnp.stack([lax.axis_index("row") * XR, window * W - 1])
-    place, packed = lax.optimization_barrier((place, packed))
+    place, line = lax.optimization_barrier((place, line))
     rowf, colf = pl.pallas_call(
         table_kernel,
         out_shape=[
@@ -309,48 +342,45 @@
         ],
         in_specs=[smem],
         out_specs=[vmem, vmem],
-        compiler_params=pltpu.CompilerParams(vmem_limit_bytes=8 * MIB),
+        compiler_params=pltpu.CompilerParams(vmem_limit_bytes=56 * MIB),
     )(place)
 
-    column = lax.all_to_all(packed, "source", 0, 0, axis_index_groups=Z_GROUPS)
-    copies = pl.pallas_call(
-        spread_kernel,
-        out_shape=jax.ShapeDtypeStruct((16, 33, 16, 128), BF16),
-        in_specs=[vmem],
-        out_specs=vmem,
-        compiler_params=pltpu.CompilerParams(vmem_limit_bytes=4 * MIB),
-    )(column)
-    rows = lax.all_to_all(copies, ("source", "row"), 0, 0, axis_index_groups=PLANE_GROUPS)
+    copies = jnp.broadcast_to(line[None], (4, 4, 33, 16, 128))
+    rows = lax.all_to_all(copies, every, 0, 0, axis_index_groups=Y_LINES[0] + X_LINES[1])
+    rows = rows.reshape(16, 33, 16, 128)
     rows, rowf, colf, dose, focus = lax.optimization_barrier((rows, rowf, colf, dose, focus))
     own = pl.pallas_call(
         turn_kernel,
         grid=(4,),
-        out_shape=jax.ShapeDtypeStruct((8, 4, 128, 256), BF16),
-        in_specs=[pl.BlockSpec((16, 8, 16, 128), lambda i: (0, i, 0, 0))],
-        out_specs=pl.BlockSpec((2, 4, 128, 256), lambda i: (i, 0, 0, 0)),
+        out_shape=jax.ShapeDtypeStruct((32, 128, 256), BF16),
+        in_specs=[smem, pl.BlockSpec((16, 8, 16, 128), lambda i: (0, i, 0, 0))],
+        out_specs=pl.BlockSpec((8, 128, 256), lambda i: (i, 0, 0)),
         compiler_params=pltpu.CompilerParams(vmem_limit_bytes=8 * MIB),
-    )(rows)
-    own = own.reshape(32, 128, 256)
-    other = lax.ppermute(own, "cond", swap)
-
-    info = lax.dynamic_slice(rows, (8 * core, 32, 0, 0), (8, 1, 8, 48))[::4, 0].astype(F32)
+    )(core.reshape(1), rows)
+    other = lax.ppermute(rows, "cond", swap)
+
+    tiles = rows[:5, 32, :8, :48]
+    info = jnp.stack([jnp.where(core == 0, tiles[0], tiles[2]), jnp.where(core == 0, tiles[4], tiles[3])]).astype(F32)
     info = (info[:, :, :16] + info[:, :, 16:32] + info[:, :, 32:]).reshape(-1)
     keep, send = pl.pallas_call(
         image_kernel,
         out_shape=[jax.ShapeDtypeStruct((8, PART_ROWS, XR), F32)] * 2,
-        in_specs=[smem] * 4 + [hbm] * 2 + [vmem] * 2,
+        in_specs=[smem] * 4 + [hbm] * 4,
         out_specs=[vmem] * 2,
         scratch_shapes=[
+            pltpu.VMEM((16, 33, 16, 128), BF16),
             pltpu.VMEM((64, 128, 256), BF16),
+            pltpu.VMEM((NB, 2 * BLOCK, 2 * XR), BF16),
+            pltpu.VMEM((NB + 1, 4, 2 * ROWS, BLOCK), BF16),
             pltpu.VMEM((LOCAL + 1, 4, 256, 256), BF16),
             pltpu.VMEM((8, ROWS, XR), F32),
             pltpu.VMEM((4, 2 * ROWS, 256), F32),
             pltpu.VMEM((4, 2 * ROWS, 256), F32),
         ] + [pltpu.VMEM((ENTRIES, BLOCK), F32)] * 5 + [
             pltpu.SMEM((ENTRIES + GROUP,), jnp.int32),
-            pltpu.SemaphoreType.DMA((2,)),
+            pltpu.SemaphoreType.DMA((4,)),
         ],
-        compiler_params=pltpu.CompilerParams(vmem_limit_bytes=24 * MIB),
+        compiler_params=pltpu.CompilerParams(vmem_limit_bytes=56 * MIB),
     )(info, info.astype(jnp.int32), focus.reshape(1), core.reshape(1), own, other, rowf, colf)
     received = lax.ppermute(send, "cond", swap)
     terms = pl.pallas_call(

time: 98.5 us -> 95.1 us (0.965)
  waiting for transfers between devices: 22 us -> 13.8 us
  Pallas kernels: 18.8 us -> 22.8 us
  other arithmetic: 0.37 us -> 1.47 us
    all_to_all x1 -> x2, waiting for transfers between devices: 16.2 us -> 10.7 us  [the longest x1 6.43 us: on_device(): lax.all_to_all(copies, every, 0, 0, axis_index_groups=X_LINES[0] + Y_LINE...]
    pallas_call x1, Pallas kernels: 11.6 us -> 15 us  [on_device(): pl.pallas_call(image_kernel, out_shape=[jax.ShapeDtypeStruct((8, PART_ROW...]
    ppermute x1, waiting for transfers between devices: 3.95 us -> 0.62 us  [on_device(): other = lax.ppermute(rows, 'cond', swap)]
    broadcast_in_dim x0 -> x1, local copies, waits for them, and re-layouts: none -> 1.64 us  [on_device(): copies = jnp.broadcast_to(line[None], (4, 4, 33, 16, 128))]
    ppermute x1, starting transfers between devices: 1.56 us -> 0.09 us  [on_device(): received = lax.ppermute(send, 'cond', swap)]
    all_to_all x1 -> x2, starting transfers between devices: 6.89 us -> 8.33 us  [the longest x1 4.18 us: on_device(): lax.all_to_all(copies, every, 0, 0, axis_index_groups=X_LINES[0] + Y_LINE...]
    ppermute x1, starting transfers between devices: 2.88 us -> 4.31 us  [on_device(): remote = lax.ppermute(local, 'cond', swap)]
    pallas_call x1, Pallas kernels: 2.61 us -> 4.01 us  [on_device(): pl.pallas_call(table_kernel, out_shape=[jax.ShapeDtypeStruct((NB, 2 * BLO...]
  transfers between devices with their start and end apart: 5 -> 6, of which waited for: 4 -> 5; matrix products, arithmetic and copies ran while one was open for 1% -> 2% of each run, Pallas kernels for 3% -> 6%
where the time goes in v2:
time: 95.1 us; the launch traced here: 95.2 us
  blocking collectives  27.8 us (29%)
  Pallas kernels  22.8 us (24%)
  starting transfers between devices  19.9 us (21%)
  waiting for transfers between devices  13.8 us (15%)
  local copies, waits for them, and re-layouts  5.35 us (6%)
  between operations  3.95 us (4%)
  other arithmetic  1.47 us (2%)
    all_to_all x1, blocking collectives, on_device(): column = lax.all_to_all(packed, 'source', 0, 0, axis_index_groups=Z_GROUPS)  17.2 us
    pallas_call x1, Pallas kernels, on_device(): pl.pallas_call(image_kernel, out_shape=[jax.ShapeDtypeStruct((8, PART_ROW...  15 us
    all_to_all x1, blocking collectives, on_device(): terms = lax.all_to_all(terms, 'source', 0, 0, axis_index_groups=TILE_GROUPS)  10.6 us
    all_to_all x1, waiting for transfers between devices, on_device(): lax.all_to_all(copies, every, 0, 0, axis_index_groups=X_LINES[0] + Y_LINE...  6.43 us
    ppermute x1, starting transfers between devices, on_device(): other = lax.ppermute(rows, 'cond', swap)  5.14 us
    ppermute x1, starting transfers between devices, on_device(): remote = lax.ppermute(local, 'cond', swap)  4.31 us
    all_to_all x1, waiting for transfers between devices, on_device(): lax.all_to_all(copies, every, 0, 0, axis_index_groups=Y_LINES[0] + X_LINE...  4.3 us
    all_to_all x1, starting transfers between devices, on_device(): lax.all_to_all(copies, every, 0, 0, axis_index_groups=X_LINES[0] + Y_LINE...  4.18 us
  transfers between devices with their start and end apart: 6, of which 5 were waited for; matrix products, arithmetic and copies ran while one was open for 2% of the time, Pallas kernels for 6%

profile of v2, /device:TPU:1, one launch (start us, length us, event | category | flops | bytes accessed | tf_op | source)
XLA Modules:
  0.0 95.2 jit_solution(15792085771285998604)
XLA Ops:
  1.3 1.6 %shard_map.73 = bf16[8,5,16,128]{3,2,1,0:T(8,128)(2,1)} custom-call(s32[1]{0:T(128)} %bitcast.2.core_ref, f32[1,2]{1,0:T(1,128)} %centers_ref.1, s32[1,1]{1,0:T(1,128)} %bitcast.28.counts_ref, f32[1,1]{1,0:T(1,128)} %bitcast.29.weights_ref, s32[1,8]{1,0:T(1,128)} %blocks_ref.1, bf16[2,8,1024]{2,1,0:T(8,128)(2,1)} %spectrum_ref.1), custom_call_target="tpu_custom_call" | custom-call | tf_op jit(solution)/shard_map/pallas_call | solution.py:308
  2.9 17.2 %all_to_all.20.column_ref = bf16[8,5,16,128]{3,2,1,0:T(8,128)(2,1)S(1)} all-to-all(bf16[8,5,16,128]{3,2,1,0:T(8,128)(2,1)} %shard_map.73), channel_id=1, replica_groups={{0,32,64,96,128,160,192,224},{8,40,72,104,136,168,200,232},{16,48,80,11..., dimensions={0} | all-to-all | bytes 327680 | tf_op jit(solution)/shard_map/all_to_all | solution.py:315
  20.0 0.9 shard_map.74
  20.9 4.2 %all-to-all-start.1 = ((bf16[4,33,16,128]{3,2,1,0:T(8,128)(2,1)}), bf16[4,33,16,128]{3,2,1,0:T(8,128)(2,1)S(1)}, u32[]{:S(2)}, u32[]{:S(2)}) async-start(bf16[4,33,16,128]{3,2,1,0:T(8,128)(2,1)} %shard_map.74), calls=%async_computation.1 | async-start | bytes 1081344 | tf_op jit(solution)/shard_map/all_to_all | solution.py:324
  25.1 0.6 pad_add_fusion.place_ref
  25.7 6.4 %all-to-all-done.1 = bf16[4,33,16,128]{3,2,1,0:T(8,128)(2,1)S(1)} async-done(((bf16[4,33,16,128]{3,2,1,0:T(8,128)(2,1)}), bf16[4,33,16,128]{3,2,1,0:T(8,128)(2,1)S(1)}, u32[]{:S(2)}, u32[]{:S(2)}) %all-to-all-start.1) | async-done | bytes 540704 | tf_op jit(solution)/shard_map/all_to_all | solution.py:324
  32.1 1.6 %broadcast_in_dim.2 = bf16[4,4,33,16,128]{4,3,2,1,0:T(8,128)(2,1)} broadcast(bf16[4,33,16,128]{3,2,1,0:T(8,128)(2,1)S(1)} %all-to-all-done.1), dimensions={1,2,3,4} | broadcast | bytes 2703360 | tf_op jit(solution)/shard_map/broadcast_in_dim | solution.py:348
  33.8 0.0 copy-start.3
  33.8 0.0 copy-start.4
  33.8 4.1 %all-to-all-start.2 = ((bf16[4,4,33,16,128]{4,3,2,1,0:T(8,128)(2,1)}), bf16[4,4,33,16,128]{4,3,2,1,0:T(8,128)(2,1)S(1)}, u32[]{:S(2)}, u32[]{:S(2)}) async-start(bf16[4,4,33,16,128]{4,3,2,1,0:T(8,128)(2,1)} %broadcast_in_dim.2), calls=%async_computation.2 | async-start | bytes 4325376 | tf_op jit(solution)/shard_map/all_to_all | solution.py:349
  37.9 0.0 copy-done.3
  37.9 0.0 copy-done.4
  37.9 0.1 pad_maximum_fusion.1
  38.0 4.3 %collective-permute-start = (f32[4]{0:T(128)S(1)}, f32[4]{0:T(128)S(1)}, u32[]{:S(2)}, u32[]{:S(2)}) collective-permute-start(f32[4]{0:T(128)S(1)} %pad_maximum_fusion.1), channel_id=1, source_target_pairs={{0,1},{1,0},{2,3},{3,2},{4,5},{5,4},{6,7},{7,6},{8,9},{9,8},{10,11... | collective-permute-start | bytes 56 | tf_op jit(solution)/shard_map/ppermute | solution.py:328
  42.3 4.0 %shard_map.75 = (bf16[8,256,256]{2,1,0:T(8,128)(2,1)}, bf16[9,4,144,128]{3,2,1,0:T(8,128)(2,1)}) custom-call(s32[2]{0:T(128)} %pad_add_fusion.place_ref), custom_call_target="tpu_custom_call" | custom-call | tf_op jit(solution)/shard_map/pallas_call | solution.py:337
  46.3 0.0 collective-permute-done
  46.3 0.1 broadcast_select_fusion
  46.4 0.7 fusion
  49.6 4.3 %all-to-all-done.2 = bf16[4,4,33,16,128]{4,3,2,1,0:T(8,128)(2,1)S(1)} async-done(((bf16[4,4,33,16,128]{4,3,2,1,0:T(8,128)(2,1)}), bf16[4,4,33,16,128]{4,3,2,1,0:T(8,128)(2,1)S(1)}, u32[]{:S(2)}, u32[]{:S(2)}) %all-to-all-start.2) | async-done | bytes 2162720 | tf_op jit(solution)/shard_map/all_to_all | solution.py:349
  53.9 5.1 %collective-permute-start.1 = (bf16[16,33,16,128]{3,2,1,0:T(8,128)(2,1)S(1)}, bf16[16,33,16,128]{3,2,1,0:T(8,128)(2,1)}, u32[]{:S(2)}, u32[]{:S(2)}) collective-permute-start(bf16[16,33,16,128]{3,2,1,0:T(8,128)(2,1)S(1)} %bitcast.30), channel_id=1, source_target_pairs={{0,1},{1,0},{2,3},{3,2},{4,5},{5,4},{6,7},{7,6},{8,9},{9,8},{10,11... | collective-permute-start | bytes 6488072 | tf_op jit(solution)/shard_map/ppermute | solution.py:360
  59.1 1.3 %shard_map.76.own_ref = bf16[32,128,256]{2,1,0:T(8,128)(2,1)S(1)} custom-call(s32[1]{0:T(128)} %bitcast.2.core_ref, bf16[16,33,16,128]{3,2,1,0:T(8,128)(2,1)S(1)} %bitcast.31), custom_call_target="tpu_custom_call" | custom-call | tf_op jit(solution)/shard_map/pallas_call | solution.py:352
  60.4 0.0 copy-start
  60.4 1.3 %copy-done = bf16[32,128,256]{2,1,0:T(8,128)(2,1)} copy-done((bf16[32,128,256]{2,1,0:T(8,128)(2,1)}, bf16[32,128,256]{2,1,0:T(8,128)(2,1)S(1)}, u32[]{:S(2)}) %copy-start) | copy-done | bytes 2097176
  61.7 0.1 slice_add_fusion
  61.8 0.1 reshape.81.info_ref
  61.9 0.0 copy-start.2
  61.9 0.6 convert_element_type.7.whole_ref
  62.5 0.6 collective-permute-done.1.other_ref
  63.1 0.0 copy-done.2
  63.1 15.0 %shard_map.77 = (f32[8,40,128]{2,1,0:T(8,128)}, f32[8,40,128]{2,1,0:T(8,128)}) custom-call(f32[256]{0:T(256)} %copy-done.2, s32[256]{0:T(256)} %convert_element_type.7.whole_ref, f32[1]{0:T(128)} %bitcast.13.focus_ref, s32[1]{0:T(128)} %bitcast.2.core_ref, bf16[32,128,256]{2,1,0:T(8,128)(2,1)} %copy-done, ...), custom_call_target="tpu_custom_call" | custom-call | tf_op jit(solution)/shard_map/pallas_call | solution.py:365
  78.1 0.1 collective-permute-start.2
  78.2 1.6 %collective-permute-done.2.other_ref = f32[8,40,128]{2,1,0:T(8,128)S(1)} collective-permute-done((f32[8,40,128]{2,1,0:T(8,128)}, f32[8,40,128]{2,1,0:T(8,128)S(1)}, u32[]{:S(2)}, u32[]{:S(2)}) %collective-permute-start.2) | collective-permute-done | bytes 163872 | tf_op jit(solution)/shard_map/ppermute | solution.py:385
  79.7 0.0 copy-start.1
  79.7 0.9 copy-done.1
  80.7 0.1 shard_map.78
  80.8 10.6 %all_to_all.21 = f32[8,32,128]{2,1,0:T(8,128)S(1)} all-to-all(f32[8,32,128]{2,1,0:T(8,128)S(1)} %shard_map.78), channel_id=1, replica_groups={{0,56,64,120,128,184,192,248},{8,48,72,112,136,176,200,240},{16,40,80,1..., dimensions={0} | all-to-all | bytes 262144 | tf_op jit(solution)/shard_map/all_to_all | solution.py:393
  91.4 2.1 %collective-permute-start.3 = (f32[2,32,128]{2,1,0:T(8,128)S(1)}, f32[2,32,128]{2,1,0:T(8,128)S(1)}, u32[]{:S(2)}, u32[]{:S(2)}) collective-permute-start(f32[2,32,128]{2,1,0:T(8,128)S(1)} %log_multiply_fusion), channel_id=1, source_target_pairs={{0,1},{1,0},{2,3},{3,2},{4,5},{5,4},{6,7},{7,6},{8,9},{9,8},{10,11... | collective-permute-start | bytes 98312 | tf_op jit(solution)/shard_map/ppermute | solution.py:395
  93.5 0.9 collective-permute-done.3
  94.4 0.7 copy.10
  (8 shorter events, 0.1 us)
Async XLA Ops:
  20.9 11.2 %all-to-all-start.1 = ((bf16[4,33,16,128]{3,2,1,0:T(8,128)(2,1)}), bf16[4,33,16,128]{3,2,1,0:T(8,128)(2,1)S(1)}, u32[]{:S(2)}, u32[]{:S(2)}) async-start(bf16[4,33,16,128]{3,2,1,0:T(8,128)(2,1)} %shard_map.74), calls=%async_computation.1 | async-start | bytes 1081344 | tf_op jit(solution)/shard_map/all_to_all | solution.py:324
  33.8 4.2 %copy-start.3 = (f32[2]{0:T(128)S(1)}, f32[2]{0:T(128)}, u32[]{:S(2)}) copy-start(f32[2]{0:T(128)} %param.13) | copy-start | bytes 28
  33.8 4.2 %copy-start.4 = (f32[2]{0:T(128)S(1)}, f32[2]{0:T(128)}, u32[]{:S(2)}) copy-start(f32[2]{0:T(128)} %param.12) | copy-start | bytes 28
  33.8 20.2 %all-to-all-start.2 = ((bf16[4,4,33,16,128]{4,3,2,1,0:T(8,128)(2,1)}), bf16[4,4,33,16,128]{4,3,2,1,0:T(8,128)(2,1)S(1)}, u32[]{:S(2)}, u32[]{:S(2)}) async-start(bf16[4,4,33,16,128]{4,3,2,1,0:T(8,128)(2,1)} %broadcast_in_dim.2), calls=%async_computation.2 | async-start | bytes 4325376 | tf_op jit(solution)/shard_map/all_to_all | solution.py:349
  38.0 8.3 %collective-permute-start = (f32[4]{0:T(128)S(1)}, f32[4]{0:T(128)S(1)}, u32[]{:S(2)}, u32[]{:S(2)}) collective-permute-start(f32[4]{0:T(128)S(1)} %pad_maximum_fusion.1), channel_id=1, source_target_pairs={{0,1},{1,0},{2,3},{3,2},{4,5},{5,4},{6,7},{7,6},{8,9},{9,8},{10,11... | collective-permute-start | bytes 56 | tf_op jit(solution)/shard_map/ppermute | solution.py:328
  53.9 9.2 %collective-permute-start.1 = (bf16[16,33,16,128]{3,2,1,0:T(8,128)(2,1)S(1)}, bf16[16,33,16,128]{3,2,1,0:T(8,128)(2,1)}, u32[]{:S(2)}, u32[]{:S(2)}) collective-permute-start(bf16[16,33,16,128]{3,2,1,0:T(8,128)(2,1)S(1)} %bitcast.30), channel_id=1, source_target_pairs={{0,1},{1,0},{2,3},{3,2},{4,5},{5,4},{6,7},{7,6},{8,9},{9,8},{10,11... | collective-permute-start | bytes 6488072 | tf_op jit(solution)/shard_map/ppermute | solution.py:360
  60.4 1.3 %copy-start = (bf16[32,128,256]{2,1,0:T(8,128)(2,1)}, bf16[32,128,256]{2,1,0:T(8,128)(2,1)S(1)}, u32[]{:S(2)}) copy-start(bf16[32,128,256]{2,1,0:T(8,128)(2,1)S(1)} %shard_map.76.own_ref) | copy-start | bytes 6291460
  61.9 1.2 %copy-start.2 = (f32[256]{0:T(256)}, f32[256]{0:T(256)S(1)}, u32[]{:S(2)}) copy-start(f32[256]{0:T(256)S(1)} %reshape.81.info_ref) | copy-start | bytes 3076
  78.1 1.7 %collective-permute-start.2 = (f32[8,40,128]{2,1,0:T(8,128)}, f32[8,40,128]{2,1,0:T(8,128)S(1)}, u32[]{:S(2)}, u32[]{:S(2)}) collective-permute-start(f32[8,40,128]{2,1,0:T(8,128)} %get-tuple-element.32), channel_id=1, source_target_pairs={{0,1},{1,0},{2,3},{3,2},{4,5},{5,4},{6,7},{7,6},{8,9},{9,8},{10,11... | collective-permute-start | bytes 491528 | tf_op jit(solution)/shard_map/ppermute | solution.py:385
  79.7 0.9 copy-start.1
  91.4 2.9 %collective-permute-start.3 = (f32[2,32,128]{2,1,0:T(8,128)S(1)}, f32[2,32,128]{2,1,0:T(8,128)S(1)}, u32[]{:S(2)}, u32[]{:S(2)}) collective-permute-start(f32[2,32,128]{2,1,0:T(8,128)S(1)} %log_multiply_fusion), channel_id=1, source_target_pairs={{0,1},{1,0},{2,3},{3,2},{4,5},{5,4},{6,7},{7,6},{8,9},{9,8},{10,11... | collective-permute-start | bytes 98312 | tf_op jit(solution)/shard_map/ppermute | solution.py:395

commit v3 on v2

--- a/solution.py
+++ b/solution.py
@@ -149,7 +149,7 @@
 
 def image_kernel(
     info_ref, whole_ref, focus_ref, core_ref, own_ref, other_ref, rows_ref, columns_ref,
-    keep_ref, send_ref, raw, turned, rowf_ref, colf_ref, pieces, power, even, odd, numbers, p_re, p_im, q_re, q_im, listing, sems,
+    keep_ref, send_ref, raw, turned, rowf_ref, colf_ref, pieces, power, even, odd, numbers, center_u, center_v, p_re, p_im, q_re, q_im, listing, sems,
 ):
     def count_of(s):
         return whole_ref[16 * s + 2]
@@ -172,26 +172,32 @@
         copy.start()
 
     def live(s, total):
+        rows = pl.ds(total, SLOTS)
+        center_u[rows, :] = jnp.full((SLOTS, BLOCK), info_ref[16 * s])
+        center_v[rows, :] = jnp.full((SLOTS, BLOCK), info_ref[16 * s + 1])
         for k in range(SLOTS):
             listing[total + k] = s * SLOTS + k
+            numbers[pl.ds(total + k, 1), :] = jnp.full((1, BLOCK), info_ref[16 * s + 4 + k])
         return total + count_of(s)
 
     total = lax.fori_loop(0, LOCAL, live, 0)
     for n in range(GROUP):
         listing[total + n] = ENTRIES
     groups = (total + GROUP - 1) >> 4
-    lane = lax.broadcasted_iota(jnp.int32, (SLOTS, BLOCK), 1)
+    lane = lax.broadcasted_iota(jnp.int32, (GROUP, BLOCK), 1)
     by_residue = ((lane & 31) * 4 + (lane >> 5)).astype(F32)
     lane = lane.astype(F32)
-    for s in range(LOCAL):
-        rows = slice(SLOTS * s, SLOTS * s + SLOTS)
-        for k in range(SLOTS):
-            numbers[SLOTS * s + k:SLOTS * s + k + 1, :] = jnp.full((1, BLOCK), info_ref[16 * s + 4 + k])
+
+    def factors(g, carry):
+        rows = pl.ds(pl.multiple_of(GROUP * g, GROUP), GROUP)
         number = numbers[rows, :]
         i = jnp.floor(number * (1.0 / NB))
         j = number - i * NB
-        p_re[rows, :], p_im[rows, :] = pupil_factor(i * BLOCK + lane - info_ref[16 * s], focus_ref[0])
-        q_re[rows, :], q_im[rows, :] = pupil_factor(j * BLOCK + by_residue - info_ref[16 * s + 1], focus_ref[0])
+        p_re[rows, :], p_im[rows, :] = pupil_factor(i * BLOCK + lane - center_u[rows, :], focus_ref[0])
+        q_re[rows, :], q_im[rows, :] = pupil_factor(j * BLOCK + by_residue - center_v[rows, :], focus_ref[0])
+        return carry
+
+    lax.fori_loop(0, groups, factors, 0)
 
     pieces[...] = jnp.zeros_like(pieces)
     power[...] = jnp.zeros_like(power)
@@ -210,15 +216,15 @@
     def entries(g, carry):
         places = [listing[g * GROUP + n] for n in range(GROUP)]
         sources = [jnp.minimum(e, ENTRIES - 1) for e in places]
-        q_all = jnp.transpose(
-            jnp.concatenate([part[pl.ds(e, 1), :] for part in (q_re, q_im) for e in sources], axis=0)
-        )
+        rows = pl.ds(pl.multiple_of(GROUP * g, GROUP), GROUP)
+        pr_all, pi_all = p_re[rows, :], p_im[rows, :]
+        q_all = jnp.transpose(jnp.concatenate([q_re[rows, :], q_im[rows, :]], axis=0))
         for n in range(GROUP):
             number = block_of(sources[n])
             i, j = number >> 3, number & 7
             block = turned[(((j >> 2) ^ core_ref[0]) << 5) + (i << 2) + (j & 3)].astype(F32)
             re, im = block[:, :128], block[:, 128:]
-            pr, pi = p_re[pl.ds(sources[n], 1), :], p_im[pl.ds(sources[n], 1), :]
+            pr, pi = pr_all[n:n + 1], pi_all[n:n + 1]
             qr, qi = q_all[:, n:n + 1], q_all[:, GROUP + n:GROUP + n + 1]
             pupil_re = qr * pr - qi * pi
             pupil_im = qr * pi + qi * pr
@@ -376,11 +382,11 @@
             pltpu.VMEM((8, ROWS, XR), F32),
             pltpu.VMEM((4, 2 * ROWS, 256), F32),
             pltpu.VMEM((4, 2 * ROWS, 256), F32),
-        ] + [pltpu.VMEM((ENTRIES, BLOCK), F32)] * 5 + [
+        ] + [pltpu.VMEM((ENTRIES + SLOTS, BLOCK), F32)] * 7 + [
             pltpu.SMEM((ENTRIES + GROUP,), jnp.int32),
             pltpu.SemaphoreType.DMA((4,)),
         ],
-        compiler_params=pltpu.CompilerParams(vmem_limit_bytes=56 * MIB),
+        compiler_params=pltpu.CompilerParams(vmem_limit_bytes=52 * MIB),
     )(info, info.astype(jnp.int32), focus.reshape(1), core.reshape(1), own, other, rowf, colf)
     received = lax.ppermute(send, "cond", swap)
     terms = pl.pallas_call(

time: 95.1 us -> 92.2 us (0.970)
  Pallas kernels: 22.8 us -> 19.5 us
  starting transfers between devices: 19.9 us -> 21.4 us
    pallas_call x1, Pallas kernels: 15 us -> 11.6 us  [on_device(): pl.pallas_call(image_kernel, out_shape=[jax.ShapeDtypeStruct((8, PART_ROW...]
    ppermute x1, starting transfers between devices: 0.09 us -> 1.51 us  [on_device(): received = lax.ppermute(send, 'cond', swap)]
    unnamed x10 -> x8, local copies, waits for them, and re-layouts: 2.23 us -> 1.32 us
where the time goes in v3:
time: 92.2 us; the launch traced here: 91.7 us
  blocking collectives  27.8 us (30%)
  starting transfers between devices  21.4 us (23%)
  Pallas kernels  19.5 us (21%)
  waiting for transfers between devices  14 us (15%)
  local copies, waits for them, and re-layouts  4.45 us (5%)
  between operations  3.74 us (4%)
    all_to_all x1, blocking collectives, on_device(): column = lax.all_to_all(packed, 'source', 0, 0, axis_index_groups=Z_GROUPS)  17.2 us
    pallas_call x1, Pallas kernels, on_device(): pl.pallas_call(image_kernel, out_shape=[jax.ShapeDtypeStruct((8, PART_ROW...  11.6 us
    all_to_all x1, blocking collectives, on_device(): terms = lax.all_to_all(terms, 'source', 0, 0, axis_index_groups=TILE_GROUPS)  10.6 us
    all_to_all x1, waiting for transfers between devices, on_device(): lax.all_to_all(copies, every, 0, 0, axis_index_groups=X_LINES[0] + Y_LINE...  6.44 us
    ppermute x1, starting transfers between devices, on_device(): other = lax.ppermute(rows, 'cond', swap)  5.14 us
    all_to_all x1, waiting for transfers between devices, on_device(): lax.all_to_all(copies, every, 0, 0, axis_index_groups=Y_LINES[0] + X_LINE...  4.49 us
    ppermute x1, starting transfers between devices, on_device(): remote = lax.ppermute(local, 'cond', swap)  4.31 us
    all_to_all x1, starting transfers between devices, on_device(): lax.all_to_all(copies, every, 0, 0, axis_index_groups=X_LINES[0] + Y_LINE...  4.18 us
  transfers between devices with their start and end apart: 6, of which 5 were waited for; matrix products, arithmetic and copies ran while one was open for 2% of the time, Pallas kernels for 6%

profile of v3, /device:TPU:1, one launch (start us, length us, event | category | flops | bytes accessed | tf_op | source)
XLA Modules:
  0.0 91.7 jit_solution(17031851808026668314)
XLA Ops:
  1.3 1.6 %shard_map.73 = bf16[8,5,16,128]{3,2,1,0:T(8,128)(2,1)} custom-call(s32[1]{0:T(128)} %bitcast.2.core_ref, f32[1,2]{1,0:T(1,128)} %centers_ref.1, s32[1,1]{1,0:T(1,128)} %bitcast.28.counts_ref, f32[1,1]{1,0:T(1,128)} %bitcast.29.weights_ref, s32[1,8]{1,0:T(1,128)} %blocks_ref.1, bf16[2,8,1024]{2,1,0:T(8,128)(2,1)} %spectrum_ref.1), custom_call_target="tpu_custom_call" | custom-call | tf_op jit(solution)/shard_map/pallas_call | solution.py:314
  2.9 17.2 %all_to_all.20.column_ref = bf16[8,5,16,128]{3,2,1,0:T(8,128)(2,1)S(1)} all-to-all(bf16[8,5,16,128]{3,2,1,0:T(8,128)(2,1)} %shard_map.73), channel_id=1, replica_groups={{0,32,64,96,128,160,192,224},{8,40,72,104,136,168,200,232},{16,48,80,11..., dimensions={0} | all-to-all | bytes 327680 | tf_op jit(solution)/shard_map/all_to_all | solution.py:321
  20.0 0.9 shard_map.74
  20.9 4.2 %all-to-all-start.1 = ((bf16[4,33,16,128]{3,2,1,0:T(8,128)(2,1)}), bf16[4,33,16,128]{3,2,1,0:T(8,128)(2,1)S(1)}, u32[]{:S(2)}, u32[]{:S(2)}) async-start(bf16[4,33,16,128]{3,2,1,0:T(8,128)(2,1)} %shard_map.74), calls=%async_computation.1 | async-start | bytes 1081344 | tf_op jit(solution)/shard_map/all_to_all | solution.py:330
  25.1 0.6 pad_add_fusion.place_ref
  25.7 6.4 %all-to-all-done.1 = bf16[4,33,16,128]{3,2,1,0:T(8,128)(2,1)S(1)} async-done(((bf16[4,33,16,128]{3,2,1,0:T(8,128)(2,1)}), bf16[4,33,16,128]{3,2,1,0:T(8,128)(2,1)S(1)}, u32[]{:S(2)}, u32[]{:S(2)}) %all-to-all-start.1) | async-done | bytes 540704 | tf_op jit(solution)/shard_map/all_to_all | solution.py:330
  32.1 1.6 %broadcast_in_dim.2 = bf16[4,4,33,16,128]{4,3,2,1,0:T(8,128)(2,1)} broadcast(bf16[4,33,16,128]{3,2,1,0:T(8,128)(2,1)S(1)} %all-to-all-done.1), dimensions={1,2,3,4} | broadcast | bytes 2703360 | tf_op jit(solution)/shard_map/broadcast_in_dim | solution.py:354
  33.8 0.0 copy-start.2
  33.8 0.0 copy-start.3
  33.8 4.1 %all-to-all-start.2 = ((bf16[4,4,33,16,128]{4,3,2,1,0:T(8,128)(2,1)}), bf16[4,4,33,16,128]{4,3,2,1,0:T(8,128)(2,1)S(1)}, u32[]{:S(2)}, u32[]{:S(2)}) async-start(bf16[4,4,33,16,128]{4,3,2,1,0:T(8,128)(2,1)} %broadcast_in_dim.2), calls=%async_computation.2 | async-start | bytes 4325376 | tf_op jit(solution)/shard_map/all_to_all | solution.py:355
  37.9 0.0 copy-done.2
  37.9 0.0 copy-done.3
  37.9 0.1 pad_maximum_fusion.1
  38.0 4.3 %collective-permute-start = (f32[4]{0:T(128)S(1)}, f32[4]{0:T(128)S(1)}, u32[]{:S(2)}, u32[]{:S(2)}) collective-permute-start(f32[4]{0:T(128)S(1)} %pad_maximum_fusion.1), channel_id=1, source_target_pairs={{0,1},{1,0},{2,3},{3,2},{4,5},{5,4},{6,7},{7,6},{8,9},{9,8},{10,11... | collective-permute-start | bytes 56 | tf_op jit(solution)/shard_map/ppermute | solution.py:334
  42.3 4.0 %shard_map.75 = (bf16[8,256,256]{2,1,0:T(8,128)(2,1)}, bf16[9,4,144,128]{3,2,1,0:T(8,128)(2,1)}) custom-call(s32[2]{0:T(128)} %pad_add_fusion.place_ref), custom_call_target="tpu_custom_call" | custom-call | tf_op jit(solution)/shard_map/pallas_call | solution.py:343
  46.3 0.0 collective-permute-done
  46.3 0.1 broadcast_select_fusion
  46.4 0.7 fusion
  49.4 4.5 %all-to-all-done.2 = bf16[4,4,33,16,128]{4,3,2,1,0:T(8,128)(2,1)S(1)} async-done(((bf16[4,4,33,16,128]{4,3,2,1,0:T(8,128)(2,1)}), bf16[4,4,33,16,128]{4,3,2,1,0:T(8,128)(2,1)S(1)}, u32[]{:S(2)}, u32[]{:S(2)}) %all-to-all-start.2) | async-done | bytes 2162720 | tf_op jit(solution)/shard_map/all_to_all | solution.py:355
  53.9 5.1 %collective-permute-start.1 = (bf16[16,33,16,128]{3,2,1,0:T(8,128)(2,1)S(1)}, bf16[16,33,16,128]{3,2,1,0:T(8,128)(2,1)}, u32[]{:S(2)}, u32[]{:S(2)}) collective-permute-start(bf16[16,33,16,128]{3,2,1,0:T(8,128)(2,1)S(1)} %bitcast.30), channel_id=1, source_target_pairs={{0,1},{1,0},{2,3},{3,2},{4,5},{5,4},{6,7},{7,6},{8,9},{9,8},{10,11... | collective-permute-start | bytes 6488072 | tf_op jit(solution)/shard_map/ppermute | solution.py:366
  59.1 0.0 copy-start.1
  59.1 1.3 %shard_map.76.own_ref = bf16[32,128,256]{2,1,0:T(8,128)(2,1)S(1)} custom-call(s32[1]{0:T(128)} %bitcast.2.core_ref, bf16[16,33,16,128]{3,2,1,0:T(8,128)(2,1)S(1)} %bitcast.31), custom_call_target="tpu_custom_call" | custom-call | tf_op jit(solution)/shard_map/pallas_call | solution.py:358
  60.4 0.0 copy-start
  60.4 1.3 %copy-done = bf16[32,128,256]{2,1,0:T(8,128)(2,1)} copy-done((bf16[32,128,256]{2,1,0:T(8,128)(2,1)}, bf16[32,128,256]{2,1,0:T(8,128)(2,1)S(1)}, u32[]{:S(2)}) %copy-start) | copy-done | bytes 2097176
  61.7 0.1 slice_add_fusion
  61.8 0.1 reshape.81.info_ref
  61.9 1.2 %collective-permute-done.1.other_ref = bf16[16,33,16,128]{3,2,1,0:T(8,128)(2,1)} collective-permute-done((bf16[16,33,16,128]{3,2,1,0:T(8,128)(2,1)S(1)}, bf16[16,33,16,128]{3,2,1,0:T(8,128)(2,1)}, u32[]{:S(2)}, u32[]{:S(2)}) %collective-permute-start.1) | collective-permute-done | bytes 2162720 | tf_op jit(solution)/shard_map/ppermute | solution.py:366
  63.1 0.0 copy-done.1
  63.1 11.6 %shard_map.77 = (f32[8,40,128]{2,1,0:T(8,128)S(1)}, f32[8,40,128]{2,1,0:T(8,128)S(1)}) custom-call(f32[256]{0:T(256)S(1)} %reshape.81.info_ref, s32[256]{0:T(256)S(1)} %convert_element_type.7.whole_ref, f32[1]{0:T(128)} %bitcast.13.focus_ref, s32[1]{0:T(128)} %bitcast.2.core_ref, bf16[32,128,256]{2,1,0:T(8,128)(2,1)} %copy-done, ...), custom_call_target="tpu_custom_call" | custom-call | tf_op jit(solution)/shard_map/pallas_call | solution.py:371
  74.7 1.5 %collective-permute-start.2 = (f32[8,40,128]{2,1,0:T(8,128)S(1)}, f32[8,40,128]{2,1,0:T(8,128)S(1)}, u32[]{:S(2)}, u32[]{:S(2)}) collective-permute-start(f32[8,40,128]{2,1,0:T(8,128)S(1)} %get-tuple-element.32), channel_id=1, source_target_pairs={{0,1},{1,0},{2,3},{3,2},{4,5},{5,4},{6,7},{7,6},{8,9},{9,8},{10,11... | collective-permute-start | bytes 491528 | tf_op jit(solution)/shard_map/ppermute | solution.py:391
  76.2 1.0 %collective-permute-done.2.other_ref = f32[8,40,128]{2,1,0:T(8,128)S(1)} collective-permute-done((f32[8,40,128]{2,1,0:T(8,128)S(1)}, f32[8,40,128]{2,1,0:T(8,128)S(1)}, u32[]{:S(2)}, u32[]{:S(2)}) %collective-permute-start.2) | collective-permute-done | bytes 163872 | tf_op jit(solution)/shard_map/ppermute | solution.py:391
  77.2 0.1 shard_map.78
  77.3 10.6 %all_to_all.21 = f32[8,32,128]{2,1,0:T(8,128)S(1)} all-to-all(f32[8,32,128]{2,1,0:T(8,128)S(1)} %shard_map.78), channel_id=1, replica_groups={{0,56,64,120,128,184,192,248},{8,48,72,112,136,176,200,240},{16,40,80,1..., dimensions={0} | all-to-all | bytes 262144 | tf_op jit(solution)/shard_map/all_to_all | solution.py:399
  88.0 2.1 %collective-permute-start.3 = (f32[2,32,128]{2,1,0:T(8,128)S(1)}, f32[2,32,128]{2,1,0:T(8,128)S(1)}, u32[]{:S(2)}, u32[]{:S(2)}) collective-permute-start(f32[2,32,128]{2,1,0:T(8,128)S(1)} %log_multiply_fusion), channel_id=1, source_target_pairs={{0,1},{1,0},{2,3},{3,2},{4,5},{5,4},{6,7},{7,6},{8,9},{9,8},{10,11... | collective-permute-start | bytes 98312 | tf_op jit(solution)/shard_map/ppermute | solution.py:401
  90.0 0.9 collective-permute-done.3
  91.0 0.7 copy.10
  (9 shorter events, 0.1 us)
Async XLA Ops:
  20.9 11.2 %all-to-all-start.1 = ((bf16[4,33,16,128]{3,2,1,0:T(8,128)(2,1)}), bf16[4,33,16,128]{3,2,1,0:T(8,128)(2,1)S(1)}, u32[]{:S(2)}, u32[]{:S(2)}) async-start(bf16[4,33,16,128]{3,2,1,0:T(8,128)(2,1)} %shard_map.74), calls=%async_computation.1 | async-start | bytes 1081344 | tf_op jit(solution)/shard_map/all_to_all | solution.py:330
  33.8 4.2 %copy-start.2 = (f32[2]{0:T(128)S(1)}, f32[2]{0:T(128)}, u32[]{:S(2)}) copy-start(f32[2]{0:T(128)} %param.13) | copy-start | bytes 28
  33.8 4.2 %copy-start.3 = (f32[2]{0:T(128)S(1)}, f32[2]{0:T(128)}, u32[]{:S(2)}) copy-start(f32[2]{0:T(128)} %param.12) | copy-start | bytes 28
  33.8 20.2 %all-to-all-start.2 = ((bf16[4,4,33,16,128]{4,3,2,1,0:T(8,128)(2,1)}), bf16[4,4,33,16,128]{4,3,2,1,0:T(8,128)(2,1)S(1)}, u32[]{:S(2)}, u32[]{:S(2)}) async-start(bf16[4,4,33,16,128]{4,3,2,1,0:T(8,128)(2,1)} %broadcast_in_dim.2), calls=%async_computation.2 | async-start | bytes 4325376 | tf_op jit(solution)/shard_map/all_to_all | solution.py:355
  38.0 8.3 %collective-permute-start = (f32[4]{0:T(128)S(1)}, f32[4]{0:T(128)S(1)}, u32[]{:S(2)}, u32[]{:S(2)}) collective-permute-start(f32[4]{0:T(128)S(1)} %pad_maximum_fusion.1), channel_id=1, source_target_pairs={{0,1},{1,0},{2,3},{3,2},{4,5},{5,4},{6,7},{7,6},{8,9},{9,8},{10,11... | collective-permute-start | bytes 56 | tf_op jit(solution)/shard_map/ppermute | solution.py:334
  53.9 9.2 %collective-permute-start.1 = (bf16[16,33,16,128]{3,2,1,0:T(8,128)(2,1)S(1)}, bf16[16,33,16,128]{3,2,1,0:T(8,128)(2,1)}, u32[]{:S(2)}, u32[]{:S(2)}) collective-permute-start(bf16[16,33,16,128]{3,2,1,0:T(8,128)(2,1)S(1)} %bitcast.30), channel_id=1, source_target_pairs={{0,1},{1,0},{2,3},{3,2},{4,5},{5,4},{6,7},{7,6},{8,9},{9,8},{10,11... | collective-permute-start | bytes 6488072 | tf_op jit(solution)/shard_map/ppermute | solution.py:366
  59.1 4.0 %copy-start.1 = (bf16[8,256,256]{2,1,0:T(8,128)(2,1)S(1)}, bf16[8,256,256]{2,1,0:T(8,128)(2,1)}, u32[]{:S(2)}) copy-start(bf16[8,256,256]{2,1,0:T(8,128)(2,1)} %get-tuple-element.29.rows_ref) | copy-start | bytes 3145732
  60.4 1.3 %copy-start = (bf16[32,128,256]{2,1,0:T(8,128)(2,1)}, bf16[32,128,256]{2,1,0:T(8,128)(2,1)S(1)}, u32[]{:S(2)}) copy-start(bf16[32,128,256]{2,1,0:T(8,128)(2,1)S(1)} %shard_map.76.own_ref) | copy-start | bytes 6291460
  74.7 2.5 %collective-permute-start.2 = (f32[8,40,128]{2,1,0:T(8,128)S(1)}, f32[8,40,128]{2,1,0:T(8,128)S(1)}, u32[]{:S(2)}, u32[]{:S(2)}) collective-permute-start(f32[8,40,128]{2,1,0:T(8,128)S(1)} %get-tuple-element.32), channel_id=1, source_target_pairs={{0,1},{1,0},{2,3},{3,2},{4,5},{5,4},{6,7},{7,6},{8,9},{9,8},{10,11... | collective-permute-start | bytes 491528 | tf_op jit(solution)/shard_map/ppermute | solution.py:391
  88.0 2.9 %collective-permute-start.3 = (f32[2,32,128]{2,1,0:T(8,128)S(1)}, f32[2,32,128]{2,1,0:T(8,128)S(1)}, u32[]{:S(2)}, u32[]{:S(2)}) collective-permute-start(f32[2,32,128]{2,1,0:T(8,128)S(1)} %log_multiply_fusion), channel_id=1, source_target_pairs={{0,1},{1,0},{2,3},{3,2},{4,5},{5,4},{6,7},{7,6},{8,9},{9,8},{10,11... | collective-permute-start | bytes 98312 | tf_op jit(solution)/shard_map/ppermute | solution.py:401

commit v4 on v3

--- a/solution.py
+++ b/solution.py
@@ -319,16 +319,7 @@
         compiler_params=pltpu.CompilerParams(vmem_limit_bytes=56 * MIB),
     )(core.reshape(1), centers, counts.reshape(1, 1), weights.reshape(1, 1), blocks, spectrum)
     column = lax.all_to_all(packed, "source", 0, 0, axis_index_groups=Z_GROUPS)
-    copies = pl.pallas_call(
-        spread_kernel,
-        out_shape=jax.ShapeDtypeStruct((4, 33, 16, 128), BF16),
-        in_specs=[vmem],
-        out_specs=vmem,
-        compiler_params=pltpu.CompilerParams(vmem_limit_bytes=4 * MIB),
-    )(column)
-    every = ("source", "row", "cond")
-    line = lax.all_to_all(copies, every, 0, 0, axis_index_groups=X_LINES[0] + Y_LINES[1])
-    defocus, dose_scale, line = lax.optimization_barrier((defocus, dose_scale, line))
+    defocus, dose_scale, column = lax.optimization_barrier((defocus, dose_scale, column))
 
     local = jnp.concatenate([defocus, dose_scale])
     remote = lax.ppermute(local, "cond", swap)
@@ -339,7 +330,7 @@
     quarter = jnp.where(z % 2 == 0, y, 3 - y)
     window = 2 * quarter + z // 4
     place = jnp.stack([lax.axis_index("row") * XR, window * W - 1])
-    place, line = lax.optimization_barrier((place, line))
+    place, column = lax.optimization_barrier((place, column))
     rowf, colf = pl.pallas_call(
         table_kernel,
         out_shape=[
@@ -351,10 +342,19 @@
         compiler_params=pltpu.CompilerParams(vmem_limit_bytes=56 * MIB),
     )(place)
 
+    copies = pl.pallas_call(
+        spread_kernel,
+        out_shape=jax.ShapeDtypeStruct((4, 33, 16, 128), BF16),
+        in_specs=[vmem],
+        out_specs=vmem,
+        compiler_params=pltpu.CompilerParams(vmem_limit_bytes=4 * MIB),
+    )(column)
+    every = ("source", "row", "cond")
+    line = lax.all_to_all(copies, every, 0, 0, axis_index_groups=X_LINES[0] + Y_LINES[1])
+    line, rowf, colf, dose, focus = lax.optimization_barrier((line, rowf, colf, dose, focus))
     copies = jnp.broadcast_to(line[None], (4, 4, 33, 16, 128))
     rows = lax.all_to_all(copies, every, 0, 0, axis_index_groups=Y_LINES[0] + X_LINES[1])
     rows = rows.reshape(16, 33, 16, 128)
-    rows, rowf, colf, dose, focus = lax.optimization_barrier((rows, rowf, colf, dose, focus))
     own = pl.pallas_call(
         turn_kernel,
         grid=(4,),

time: 92.2 us -> 90.5 us (0.982)
  waiting for transfers between devices: 14 us -> 10.6 us
  blocking collectives: 27.8 us -> 31 us
  local copies, waits for them, and re-layouts: 4.45 us -> 3.09 us
  starting transfers between devices: 21.4 us -> 20.2 us
  Pallas kernels: 19.5 us -> 20.5 us
    all_to_all x1, waiting for transfers between devices: 6.44 us -> 0.01 us  [on_device(): lax.all_to_all(copies, every, 0, 0, axis_index_groups=X_LINES[0] + Y_LINE...]
    all_to_all x1, starting transfers between devices: 4.14 us -> 9.01 us  [on_device(): column = lax.all_to_all(packed, 'source', 0, 0, axis_index_groups=Z_GROUPS)]
    ppermute x1, starting transfers between devices: 5.14 us -> 1.72 us  [on_device(): other = lax.ppermute(rows, 'cond', swap)]
    all_to_all x1, blocking collectives: 17.2 us -> 20.3 us  [on_device(): lax.all_to_all(copies, every, 0, 0, axis_index_groups=Y_LINES[0] + X_LINE...]
    all_to_all x1, waiting for transfers between devices: 4.49 us -> 7.5 us  [on_device(): column = lax.all_to_all(packed, 'source', 0, 0, axis_index_groups=Z_GROUPS)]
    ppermute x1, starting transfers between devices: 4.31 us -> 2.71 us  [on_device(): remote = lax.ppermute(local, 'cond', swap)]
    broadcast_in_dim x1, local copies, waits for them, and re-layouts: 1.64 us -> 0.28 us  [on_device(): copies = jnp.broadcast_to(line[None], (4, 4, 33, 16, 128))]
    pallas_call x1, Pallas kernels: 11.6 us -> 12.6 us  [on_device(): pl.pallas_call(image_kernel, out_shape=[jax.ShapeDtypeStruct((8, PART_ROW...]
  transfers between devices with their start and end apart: 6 -> 6, of which waited for: 5 -> 4; matrix products, arithmetic and copies ran while one was open for 2% -> 2% of each run, Pallas kernels for 6% -> 6%
where the time goes in v4:
time: 90.5 us; the launch traced here: 90 us
  blocking collectives  31 us (34%)
  Pallas kernels  20.5 us (23%)
  starting transfers between devices  20.2 us (22%)
  waiting for transfers between devices  10.6 us (12%)
  between operations  3.8 us (4%)
  local copies, waits for them, and re-layouts  3.09 us (3%)
  other arithmetic  0.95 us (1%)
    all_to_all x1, blocking collectives, on_device(): lax.all_to_all(copies, every, 0, 0, axis_index_groups=Y_LINES[0] + X_LINE...  20.3 us
    pallas_call x1, Pallas kernels, on_device(): pl.pallas_call(image_kernel, out_shape=[jax.ShapeDtypeStruct((8, PART_ROW...  12.6 us
    all_to_all x1, blocking collectives, on_device(): terms = lax.all_to_all(terms, 'source', 0, 0, axis_index_groups=TILE_GROUPS)  10.6 us
    all_to_all x1, starting transfers between devices, on_device(): column = lax.all_to_all(packed, 'source', 0, 0, axis_index_groups=Z_GROUPS)  9.01 us
    all_to_all x1, waiting for transfers between devices, on_device(): column = lax.all_to_all(packed, 'source', 0, 0, axis_index_groups=Z_GROUPS)  7.5 us
    all_to_all x1, starting transfers between devices, on_device(): lax.all_to_all(copies, every, 0, 0, axis_index_groups=X_LINES[0] + Y_LINE...  4.18 us
    pallas_call x1, Pallas kernels, on_device(): pl.pallas_call(table_kernel, out_shape=[jax.ShapeDtypeStruct((NB, 2 * BLO...  4.02 us
    ppermute x1, starting transfers between devices, on_device(): remote = lax.ppermute(local, 'cond', swap)  2.71 us
  transfers between devices with their start and end apart: 6, of which 4 were waited for; matrix products, arithmetic and copies ran while one was open for 2% of the time, Pallas kernels for 6%

profile of v4, /device:TPU:1, one launch (start us, length us, event | category | flops | bytes accessed | tf_op | source)
XLA Modules:
  0.0 90.0 jit_solution(4221611034387722378)
XLA Ops:
  0.0 0.0 copy-start.3
  0.0 0.0 copy-start.2
  1.3 1.6 %shard_map.73 = bf16[8,5,16,128]{3,2,1,0:T(8,128)(2,1)} custom-call(s32[1]{0:T(128)} %bitcast.2.core_ref, f32[1,2]{1,0:T(1,128)} %centers_ref.1, s32[1,1]{1,0:T(1,128)} %bitcast.28.counts_ref, f32[1,1]{1,0:T(1,128)} %bitcast.29.weights_ref, s32[1,8]{1,0:T(1,128)} %blocks_ref.1, bf16[2,8,1024]{2,1,0:T(8,128)(2,1)} %spectrum_ref.1), custom_call_target="tpu_custom_call" | custom-call | tf_op jit(solution)/shard_map/pallas_call | solution.py:314
  2.9 9.0 %all-to-all-start = ((bf16[8,5,16,128]{3,2,1,0:T(8,128)(2,1)}), bf16[8,5,16,128]{3,2,1,0:T(8,128)(2,1)S(1)}, u32[]{:S(2)}, u32[]{:S(2)}) async-start(bf16[8,5,16,128]{3,2,1,0:T(8,128)(2,1)} %shard_map.73), calls=%async_computation | async-start | bytes 327680 | tf_op jit(solution)/shard_map/all_to_all | solution.py:321
  11.9 0.6 pad_add_fusion.place_ref
  12.6 7.5 %all-to-all-done.column_ref = bf16[8,5,16,128]{3,2,1,0:T(8,128)(2,1)S(1)} async-done(((bf16[8,5,16,128]{3,2,1,0:T(8,128)(2,1)}), bf16[8,5,16,128]{3,2,1,0:T(8,128)(2,1)S(1)}, u32[]{:S(2)}, u32[]{:S(2)}) %all-to-all-start) | async-done | bytes 163872 | tf_op jit(solution)/shard_map/all_to_all | solution.py:321
  20.1 0.9 shard_map.74
  21.0 4.2 %all-to-all-start.1 = ((bf16[4,33,16,128]{3,2,1,0:T(8,128)(2,1)}), bf16[4,33,16,128]{3,2,1,0:T(8,128)(2,1)S(1)}, u32[]{:S(2)}, u32[]{:S(2)}) async-start(bf16[4,33,16,128]{3,2,1,0:T(8,128)(2,1)} %shard_map.74), calls=%async_computation.1 | async-start | bytes 1081344 | tf_op jit(solution)/shard_map/all_to_all | solution.py:353
  25.1 0.0 copy-done.3
  25.1 0.0 copy-done.2
  25.1 0.1 pad_maximum_fusion.1
  25.2 2.7 %collective-permute-start = (f32[4]{0:T(128)S(1)}, f32[4]{0:T(128)S(1)}, u32[]{:S(2)}, u32[]{:S(2)}) collective-permute-start(f32[4]{0:T(128)S(1)} %pad_maximum_fusion.1), channel_id=1, source_target_pairs={{0,1},{1,0},{2,3},{3,2},{4,5},{5,4},{6,7},{7,6},{8,9},{9,8},{10,11... | collective-permute-start | bytes 56 | tf_op jit(solution)/shard_map/ppermute | solution.py:325
  27.9 4.0 %shard_map.75 = (bf16[8,256,256]{2,1,0:T(8,128)(2,1)}, bf16[9,4,144,128]{3,2,1,0:T(8,128)(2,1)}) custom-call(s32[2]{0:T(128)} %pad_add_fusion.place_ref), custom_call_target="tpu_custom_call" | custom-call | tf_op jit(solution)/shard_map/pallas_call | solution.py:334
  31.9 0.0 collective-permute-done
  32.0 0.1 broadcast_select_fusion
  32.0 0.7 fusion.2
  35.1 0.0 all-to-all-done.1
  35.1 0.3 broadcast_in_dim.2
  35.4 20.3 %all_to_all.20 = bf16[4,4,33,16,128]{4,3,2,1,0:T(8,128)(2,1)S(1)} all-to-all(bf16[4,4,33,16,128]{4,3,2,1,0:T(8,128)(2,1)S(1)} %broadcast_in_dim.2), channel_id=1, replica_groups={{0,8,16,24},{2,10,18,26},{4,12,20,28},{6,14,22,30},{32,40,48,56},{34,42..., dimensions={0} | all-to-all | bytes 4325376 | tf_op jit(solution)/shard_map/all_to_all | solution.py:356
  55.7 1.7 %collective-permute-start.1 = (bf16[16,33,16,128]{3,2,1,0:T(8,128)(2,1)S(1)}, bf16[16,33,16,128]{3,2,1,0:T(8,128)(2,1)}, u32[]{:S(2)}, u32[]{:S(2)}) collective-permute-start(bf16[16,33,16,128]{3,2,1,0:T(8,128)(2,1)S(1)} %bitcast.30), channel_id=1, source_target_pairs={{0,1},{1,0},{2,3},{3,2},{4,5},{5,4},{6,7},{7,6},{8,9},{9,8},{10,11... | collective-permute-start | bytes 6488072 | tf_op jit(solution)/shard_map/ppermute | solution.py:366
  57.4 0.0 copy-start.1
  57.4 1.3 %shard_map.76.own_ref = bf16[32,128,256]{2,1,0:T(8,128)(2,1)S(1)} custom-call(s32[1]{0:T(128)} %bitcast.2.core_ref, bf16[16,33,16,128]{3,2,1,0:T(8,128)(2,1)S(1)} %bitcast.31), custom_call_target="tpu_custom_call" | custom-call | tf_op jit(solution)/shard_map/pallas_call | solution.py:358
  58.7 0.0 copy-start
  58.7 1.3 %copy-done = bf16[32,128,256]{2,1,0:T(8,128)(2,1)} copy-done((bf16[32,128,256]{2,1,0:T(8,128)(2,1)}, bf16[32,128,256]{2,1,0:T(8,128)(2,1)S(1)}, u32[]{:S(2)}) %copy-start) | copy-done | bytes 2097176
  60.1 0.1 slice_add_fusion
  60.1 0.1 reshape.81.info_ref
  60.2 1.2 %collective-permute-done.1.other_ref = bf16[16,33,16,128]{3,2,1,0:T(8,128)(2,1)} collective-permute-done((bf16[16,33,16,128]{3,2,1,0:T(8,128)(2,1)S(1)}, bf16[16,33,16,128]{3,2,1,0:T(8,128)(2,1)}, u32[]{:S(2)}, u32[]{:S(2)}) %collective-permute-start.1) | collective-permute-done | bytes 2162720 | tf_op jit(solution)/shard_map/ppermute | solution.py:366
  61.4 0.0 copy-done.1
  61.4 12.6 %shard_map.77 = (f32[8,40,128]{2,1,0:T(8,128)S(1)}, f32[8,40,128]{2,1,0:T(8,128)S(1)}) custom-call(f32[256]{0:T(256)S(1)} %reshape.81.info_ref, s32[256]{0:T(256)S(1)} %convert_element_type.7.whole_ref, f32[1]{0:T(128)} %bitcast.13.focus_ref, s32[1]{0:T(128)} %bitcast.2.core_ref, bf16[32,128,256]{2,1,0:T(8,128)(2,1)} %copy-done, ...), custom_call_target="tpu_custom_call" | custom-call | tf_op jit(solution)/shard_map/pallas_call | solution.py:371
  74.0 0.5 collective-permute-start.2
  74.5 1.0 %collective-permute-done.2.other_ref = f32[8,40,128]{2,1,0:T(8,128)S(1)} collective-permute-done((f32[8,40,128]{2,1,0:T(8,128)S(1)}, f32[8,40,128]{2,1,0:T(8,128)S(1)}, u32[]{:S(2)}, u32[]{:S(2)}) %collective-permute-start.2) | collective-permute-done | bytes 163872 | tf_op jit(solution)/shard_map/ppermute | solution.py:391
  75.6 0.1 shard_map.78
  75.7 10.6 %all_to_all.21 = f32[8,32,128]{2,1,0:T(8,128)S(1)} all-to-all(f32[8,32,128]{2,1,0:T(8,128)S(1)} %shard_map.78), channel_id=1, replica_groups={{0,56,64,120,128,184,192,248},{8,48,72,112,136,176,200,240},{16,40,80,1..., dimensions={0} | all-to-all | bytes 262144 | tf_op jit(solution)/shard_map/all_to_all | solution.py:399
  86.3 2.1 %collective-permute-start.3 = (f32[2,32,128]{2,1,0:T(8,128)S(1)}, f32[2,32,128]{2,1,0:T(8,128)S(1)}, u32[]{:S(2)}, u32[]{:S(2)}) collective-permute-start(f32[2,32,128]{2,1,0:T(8,128)S(1)} %log_multiply_fusion), channel_id=1, source_target_pairs={{0,1},{1,0},{2,3},{3,2},{4,5},{5,4},{6,7},{7,6},{8,9},{9,8},{10,11... | collective-permute-start | bytes 98312 | tf_op jit(solution)/shard_map/ppermute | solution.py:401
  88.4 0.9 collective-permute-done.3
  89.3 0.7 copy.10
  (9 shorter events, 0.1 us)
Async XLA Ops:
  0.0 25.1 %copy-start.3 = (f32[2]{0:T(128)S(1)}, f32[2]{0:T(128)}, u32[]{:S(2)}) copy-start(f32[2]{0:T(128)} %param.12) | copy-start | bytes 28
  0.0 25.1 %copy-start.2 = (f32[2]{0:T(128)S(1)}, f32[2]{0:T(128)}, u32[]{:S(2)}) copy-start(f32[2]{0:T(128)} %param.13) | copy-start | bytes 28
  2.9 17.2 %all-to-all-start = ((bf16[8,5,16,128]{3,2,1,0:T(8,128)(2,1)}), bf16[8,5,16,128]{3,2,1,0:T(8,128)(2,1)S(1)}, u32[]{:S(2)}, u32[]{:S(2)}) async-start(bf16[8,5,16,128]{3,2,1,0:T(8,128)(2,1)} %shard_map.73), calls=%async_computation | async-start | bytes 327680 | tf_op jit(solution)/shard_map/all_to_all | solution.py:321
  21.0 14.1 %all-to-all-start.1 = ((bf16[4,33,16,128]{3,2,1,0:T(8,128)(2,1)}), bf16[4,33,16,128]{3,2,1,0:T(8,128)(2,1)S(1)}, u32[]{:S(2)}, u32[]{:S(2)}) async-start(bf16[4,33,16,128]{3,2,1,0:T(8,128)(2,1)} %shard_map.74), calls=%async_computation.1 | async-start | bytes 1081344 | tf_op jit(solution)/shard_map/all_to_all | solution.py:353
  25.2 6.7 %collective-permute-start = (f32[4]{0:T(128)S(1)}, f32[4]{0:T(128)S(1)}, u32[]{:S(2)}, u32[]{:S(2)}) collective-permute-start(f32[4]{0:T(128)S(1)} %pad_maximum_fusion.1), channel_id=1, source_target_pairs={{0,1},{1,0},{2,3},{3,2},{4,5},{5,4},{6,7},{7,6},{8,9},{9,8},{10,11... | collective-permute-start | bytes 56 | tf_op jit(solution)/shard_map/ppermute | solution.py:325
  55.7 5.7 %collective-permute-start.1 = (bf16[16,33,16,128]{3,2,1,0:T(8,128)(2,1)S(1)}, bf16[16,33,16,128]{3,2,1,0:T(8,128)(2,1)}, u32[]{:S(2)}, u32[]{:S(2)}) collective-permute-start(bf16[16,33,16,128]{3,2,1,0:T(8,128)(2,1)S(1)} %bitcast.30), channel_id=1, source_target_pairs={{0,1},{1,0},{2,3},{3,2},{4,5},{5,4},{6,7},{7,6},{8,9},{9,8},{10,11... | collective-permute-start | bytes 6488072 | tf_op jit(solution)/shard_map/ppermute | solution.py:366
  57.4 4.0 %copy-start.1 = (bf16[8,256,256]{2,1,0:T(8,128)(2,1)S(1)}, bf16[8,256,256]{2,1,0:T(8,128)(2,1)}, u32[]{:S(2)}) copy-start(bf16[8,256,256]{2,1,0:T(8,128)(2,1)} %get-tuple-element.29.rows_ref) | copy-start | bytes 3145732
  58.7 1.3 %copy-start = (bf16[32,128,256]{2,1,0:T(8,128)(2,1)}, bf16[32,128,256]{2,1,0:T(8,128)(2,1)S(1)}, u32[]{:S(2)}) copy-start(bf16[32,128,256]{2,1,0:T(8,128)(2,1)S(1)} %shard_map.76.own_ref) | copy-start | bytes 6291460
  74.0 1.5 %collective-permute-start.2 = (f32[8,40,128]{2,1,0:T(8,128)S(1)}, f32[8,40,128]{2,1,0:T(8,128)S(1)}, u32[]{:S(2)}, u32[]{:S(2)}) collective-permute-start(f32[8,40,128]{2,1,0:T(8,128)S(1)} %get-tuple-element.32), channel_id=1, source_target_pairs={{0,1},{1,0},{2,3},{3,2},{4,5},{5,4},{6,7},{7,6},{8,9},{9,8},{10,11... | collective-permute-start | bytes 491528 | tf_op jit(solution)/shard_map/ppermute | solution.py:391
  86.3 2.9 %collective-permute-start.3 = (f32[2,32,128]{2,1,0:T(8,128)S(1)}, f32[2,32,128]{2,1,0:T(8,128)S(1)}, u32[]{:S(2)}, u32[]{:S(2)}) collective-permute-start(f32[2,32,128]{2,1,0:T(8,128)S(1)} %log_multiply_fusion), channel_id=1, source_target_pairs={{0,1},{1,0},{2,3},{3,2},{4,5},{5,4},{6,7},{7,6},{8,9},{9,8},{10,11... | collective-permute-start | bytes 98312 | tf_op jit(solution)/shard_map/ppermute | solution.py:401

commit v5 on v4

--- a/solution.py
+++ b/solution.py
@@ -339,7 +339,7 @@
         ],
         in_specs=[smem],
         out_specs=[vmem, vmem],
-        compiler_params=pltpu.CompilerParams(vmem_limit_bytes=56 * MIB),
+        compiler_params=pltpu.CompilerParams(vmem_limit_bytes=8 * MIB),
     )(place)
 
     copies = pl.pallas_call(

time: 90.5 us -> 90.5 us (level)
  Pallas kernels: 20.5 us -> 19.1 us
  local copies, waits for them, and re-layouts: 3.09 us -> 4.2 us
    pallas_call x1, Pallas kernels: 4.02 us -> 2.61 us  [on_device(): pl.pallas_call(table_kernel, out_shape=[jax.ShapeDtypeStruct((NB, 2 * BLO...]
    unnamed x8, local copies, waits for them, and re-layouts: 1.32 us -> 2.43 us
  transfers between devices with their start and end apart: 6 -> 6, of which waited for: 4 -> 4; matrix products, arithmetic and copies ran while one was open for 2% -> 1% of each run, Pallas kernels for 6% -> 4%
where the time goes in v5:
time: 90.5 us; the launch traced here: 90 us
  blocking collectives  30.7 us (34%)
  starting transfers between devices  20.6 us (23%)
  Pallas kernels  19.1 us (21%)
  waiting for transfers between devices  11.2 us (12%)
  local copies, waits for them, and re-layouts  4.2 us (5%)
  between operations  3.89 us (4%)
    all_to_all x1, blocking collectives, on_device(): lax.all_to_all(copies, every, 0, 0, axis_index_groups=Y_LINES[0] + X_LINE...  20.1 us
    pallas_call x1, Pallas kernels, on_device(): pl.pallas_call(image_kernel, out_shape=[jax.ShapeDtypeStruct((8, PART_ROW...  12.6 us
    all_to_all x1, blocking collectives, on_device(): terms = lax.all_to_all(terms, 'source', 0, 0, axis_index_groups=TILE_GROUPS)  10.6 us
    all_to_all x1, starting transfers between devices, on_device(): column = lax.all_to_all(packed, 'source', 0, 0, axis_index_groups=Z_GROUPS)  9.01 us
    all_to_all x1, waiting for transfers between devices, on_device(): column = lax.all_to_all(packed, 'source', 0, 0, axis_index_groups=Z_GROUPS)  8.07 us
    all_to_all x1, starting transfers between devices, on_device(): lax.all_to_all(copies, every, 0, 0, axis_index_groups=X_LINES[0] + Y_LINE...  4.18 us
    ppermute x1, starting transfers between devices, on_device(): remote = lax.ppermute(local, 'cond', swap)  2.71 us
    pallas_call x1, Pallas kernels, on_device(): pl.pallas_call(table_kernel, out_shape=[jax.ShapeDtypeStruct((NB, 2 * BLO...  2.61 us
  transfers between devices with their start and end apart: 6, of which 4 were waited for; matrix products, arithmetic and copies ran while one was open for 1% of the time, Pallas kernels for 4%

profile of v5, /device:TPU:1, one launch (start us, length us, event | category | flops | bytes accessed | tf_op | source)
XLA Modules:
  0.0 90.0 jit_solution(15207034119069144798)
XLA Ops:
  0.0 0.0 copy-start.3
  0.0 0.0 copy-start.2
  1.3 1.6 %shard_map.73 = bf16[8,5,16,128]{3,2,1,0:T(8,128)(2,1)} custom-call(s32[1]{0:T(128)} %bitcast.2.core_ref, f32[1,2]{1,0:T(1,128)} %centers_ref.1, s32[1,1]{1,0:T(1,128)} %bitcast.28.counts_ref, f32[1,1]{1,0:T(1,128)} %bitcast.29.weights_ref, s32[1,8]{1,0:T(1,128)} %blocks_ref.1, bf16[2,8,1024]{2,1,0:T(8,128)(2,1)} %spectrum_ref.1), custom_call_target="tpu_custom_call" | custom-call | tf_op jit(solution)/shard_map/pallas_call | solution.py:314
  2.9 9.0 %all-to-all-start = ((bf16[8,5,16,128]{3,2,1,0:T(8,128)(2,1)}), bf16[8,5,16,128]{3,2,1,0:T(8,128)(2,1)S(1)}, u32[]{:S(2)}, u32[]{:S(2)}) async-start(bf16[8,5,16,128]{3,2,1,0:T(8,128)(2,1)} %shard_map.73), calls=%async_computation | async-start | bytes 327680 | tf_op jit(solution)/shard_map/all_to_all | solution.py:321
  11.9 0.1 pad_add_fusion.place_ref
  12.0 8.1 %all-to-all-done.column_ref = bf16[8,5,16,128]{3,2,1,0:T(8,128)(2,1)S(1)} async-done(((bf16[8,5,16,128]{3,2,1,0:T(8,128)(2,1)}), bf16[8,5,16,128]{3,2,1,0:T(8,128)(2,1)S(1)}, u32[]{:S(2)}, u32[]{:S(2)}) %all-to-all-start) | async-done | bytes 163872 | tf_op jit(solution)/shard_map/all_to_all | solution.py:321
  20.1 0.9 shard_map.74
  21.0 4.2 %all-to-all-start.1 = ((bf16[4,33,16,128]{3,2,1,0:T(8,128)(2,1)}), bf16[4,33,16,128]{3,2,1,0:T(8,128)(2,1)S(1)}, u32[]{:S(2)}, u32[]{:S(2)}) async-start(bf16[4,33,16,128]{3,2,1,0:T(8,128)(2,1)} %shard_map.74), calls=%async_computation.1 | async-start | bytes 1081344 | tf_op jit(solution)/shard_map/all_to_all | solution.py:353
  25.1 0.0 copy-done.3
  25.1 0.0 copy-done.2
  25.1 0.1 pad_maximum_fusion.1
  25.2 2.7 %collective-permute-start = (f32[4]{0:T(128)S(1)}, f32[4]{0:T(128)S(1)}, u32[]{:S(2)}, u32[]{:S(2)}) collective-permute-start(f32[4]{0:T(128)S(1)} %pad_maximum_fusion.1), channel_id=1, source_target_pairs={{0,1},{1,0},{2,3},{3,2},{4,5},{5,4},{6,7},{7,6},{8,9},{9,8},{10,11... | collective-permute-start | bytes 56 | tf_op jit(solution)/shard_map/ppermute | solution.py:325
  27.9 2.6 %shard_map.75 = (bf16[8,256,256]{2,1,0:T(8,128)(2,1)S(1)}, bf16[9,4,144,128]{3,2,1,0:T(8,128)(2,1)S(1)}) custom-call(s32[2]{0:T(128)S(1)} %pad_add_fusion.place_ref), custom_call_target="tpu_custom_call" | custom-call | tf_op jit(solution)/shard_map/pallas_call | solution.py:334
  30.5 0.0 copy-start.1
  30.6 1.1 %copy-done.1 = bf16[9,4,144,128]{3,2,1,0:T(8,128)(2,1)} copy-done((bf16[9,4,144,128]{3,2,1,0:T(8,128)(2,1)}, bf16[9,4,144,128]{3,2,1,0:T(8,128)(2,1)S(1)}, u32[]{:S(2)}) %copy-start.1) | copy-done | bytes 1327128
  31.7 0.0 collective-permute-done
  31.7 0.1 broadcast_select_fusion
  31.7 0.7 fusion.2
  34.9 0.0 all-to-all-done.1
  34.9 0.3 broadcast_in_dim.2
  35.1 20.1 %all_to_all.20 = bf16[4,4,33,16,128]{4,3,2,1,0:T(8,128)(2,1)S(1)} all-to-all(bf16[4,4,33,16,128]{4,3,2,1,0:T(8,128)(2,1)S(1)} %broadcast_in_dim.2), channel_id=1, replica_groups={{0,8,16,24},{2,10,18,26},{4,12,20,28},{6,14,22,30},{32,40,48,56},{34,42..., dimensions={0} | all-to-all | bytes 4325376 | tf_op jit(solution)/shard_map/all_to_all | solution.py:356
  55.3 2.2 %collective-permute-start.1 = (bf16[16,33,16,128]{3,2,1,0:T(8,128)(2,1)S(1)}, bf16[16,33,16,128]{3,2,1,0:T(8,128)(2,1)}, u32[]{:S(2)}, u32[]{:S(2)}) collective-permute-start(bf16[16,33,16,128]{3,2,1,0:T(8,128)(2,1)S(1)} %bitcast.30), channel_id=1, source_target_pairs={{0,1},{1,0},{2,3},{3,2},{4,5},{5,4},{6,7},{7,6},{8,9},{9,8},{10,11... | collective-permute-start | bytes 6488072 | tf_op jit(solution)/shard_map/ppermute | solution.py:366
  57.4 1.3 %shard_map.76.own_ref = bf16[32,128,256]{2,1,0:T(8,128)(2,1)S(1)} custom-call(s32[1]{0:T(128)} %bitcast.2.core_ref, bf16[16,33,16,128]{3,2,1,0:T(8,128)(2,1)S(1)} %bitcast.31), custom_call_target="tpu_custom_call" | custom-call | tf_op jit(solution)/shard_map/pallas_call | solution.py:358
  58.7 0.0 copy-start
  58.7 1.3 %copy-done = bf16[32,128,256]{2,1,0:T(8,128)(2,1)} copy-done((bf16[32,128,256]{2,1,0:T(8,128)(2,1)}, bf16[32,128,256]{2,1,0:T(8,128)(2,1)S(1)}, u32[]{:S(2)}) %copy-start) | copy-done | bytes 2097176
  60.1 0.1 slice_add_fusion
  60.1 0.1 reshape.81.info_ref
  60.2 1.2 %collective-permute-done.1.other_ref = bf16[16,33,16,128]{3,2,1,0:T(8,128)(2,1)} collective-permute-done((bf16[16,33,16,128]{3,2,1,0:T(8,128)(2,1)S(1)}, bf16[16,33,16,128]{3,2,1,0:T(8,128)(2,1)}, u32[]{:S(2)}, u32[]{:S(2)}) %collective-permute-start.1) | collective-permute-done | bytes 2162720 | tf_op jit(solution)/shard_map/ppermute | solution.py:366
  61.4 12.6 %shard_map.77 = (f32[8,40,128]{2,1,0:T(8,128)S(1)}, f32[8,40,128]{2,1,0:T(8,128)S(1)}) custom-call(f32[256]{0:T(256)S(1)} %reshape.81.info_ref, s32[256]{0:T(256)S(1)} %convert_element_type.7.whole_ref, f32[1]{0:T(128)} %bitcast.13.focus_ref, s32[1]{0:T(128)} %bitcast.2.core_ref, bf16[32,128,256]{2,1,0:T(8,128)(2,1)} %copy-done, ...), custom_call_target="tpu_custom_call" | custom-call | tf_op jit(solution)/shard_map/pallas_call | solution.py:371
  74.0 0.5 collective-permute-start.2
  74.5 1.0 %collective-permute-done.2.other_ref = f32[8,40,128]{2,1,0:T(8,128)S(1)} collective-permute-done((f32[8,40,128]{2,1,0:T(8,128)S(1)}, f32[8,40,128]{2,1,0:T(8,128)S(1)}, u32[]{:S(2)}, u32[]{:S(2)}) %collective-permute-start.2) | collective-permute-done | bytes 163872 | tf_op jit(solution)/shard_map/ppermute | solution.py:391
  75.6 0.1 shard_map.78
  75.7 10.6 %all_to_all.21 = f32[8,32,128]{2,1,0:T(8,128)S(1)} all-to-all(f32[8,32,128]{2,1,0:T(8,128)S(1)} %shard_map.78), channel_id=1, replica_groups={{0,56,64,120,128,184,192,248},{8,48,72,112,136,176,200,240},{16,40,80,1..., dimensions={0} | all-to-all | bytes 262144 | tf_op jit(solution)/shard_map/all_to_all | solution.py:399
  86.3 2.1 %collective-permute-start.3 = (f32[2,32,128]{2,1,0:T(8,128)S(1)}, f32[2,32,128]{2,1,0:T(8,128)S(1)}, u32[]{:S(2)}, u32[]{:S(2)}) collective-permute-start(f32[2,32,128]{2,1,0:T(8,128)S(1)} %log_multiply_fusion), channel_id=1, source_target_pairs={{0,1},{1,0},{2,3},{3,2},{4,5},{5,4},{6,7},{7,6},{8,9},{9,8},{10,11... | collective-permute-start | bytes 98312 | tf_op jit(solution)/shard_map/ppermute | solution.py:401
  88.4 0.9 collective-permute-done.3
  89.3 0.7 copy.10
  (9 shorter events, 0.1 us)
Async XLA Ops:
  0.0 25.1 %copy-start.3 = (f32[2]{0:T(128)S(1)}, f32[2]{0:T(128)}, u32[]{:S(2)}) copy-start(f32[2]{0:T(128)} %param.12) | copy-start | bytes 28
  0.0 25.1 %copy-start.2 = (f32[2]{0:T(128)S(1)}, f32[2]{0:T(128)}, u32[]{:S(2)}) copy-start(f32[2]{0:T(128)} %param.13) | copy-start | bytes 28
  2.9 17.2 %all-to-all-start = ((bf16[8,5,16,128]{3,2,1,0:T(8,128)(2,1)}), bf16[8,5,16,128]{3,2,1,0:T(8,128)(2,1)S(1)}, u32[]{:S(2)}, u32[]{:S(2)}) async-start(bf16[8,5,16,128]{3,2,1,0:T(8,128)(2,1)} %shard_map.73), calls=%async_computation | async-start | bytes 327680 | tf_op jit(solution)/shard_map/all_to_all | solution.py:321
  21.0 13.9 %all-to-all-start.1 = ((bf16[4,33,16,128]{3,2,1,0:T(8,128)(2,1)}), bf16[4,33,16,128]{3,2,1,0:T(8,128)(2,1)S(1)}, u32[]{:S(2)}, u32[]{:S(2)}) async-start(bf16[4,33,16,128]{3,2,1,0:T(8,128)(2,1)} %shard_map.74), calls=%async_computation.1 | async-start | bytes 1081344 | tf_op jit(solution)/shard_map/all_to_all | solution.py:353
  25.2 6.4 %collective-permute-start = (f32[4]{0:T(128)S(1)}, f32[4]{0:T(128)S(1)}, u32[]{:S(2)}, u32[]{:S(2)}) collective-permute-start(f32[4]{0:T(128)S(1)} %pad_maximum_fusion.1), channel_id=1, source_target_pairs={{0,1},{1,0},{2,3},{3,2},{4,5},{5,4},{6,7},{7,6},{8,9},{9,8},{10,11... | collective-permute-start | bytes 56 | tf_op jit(solution)/shard_map/ppermute | solution.py:325
  30.5 1.1 %copy-start.1 = (bf16[9,4,144,128]{3,2,1,0:T(8,128)(2,1)}, bf16[9,4,144,128]{3,2,1,0:T(8,128)(2,1)S(1)}, u32[]{:S(2)}) copy-start(bf16[9,4,144,128]{3,2,1,0:T(8,128)(2,1)S(1)} %get-tuple-element.30.columns_ref) | copy-start | bytes 3981316
  55.3 6.2 %collective-permute-start.1 = (bf16[16,33,16,128]{3,2,1,0:T(8,128)(2,1)S(1)}, bf16[16,33,16,128]{3,2,1,0:T(8,128)(2,1)}, u32[]{:S(2)}, u32[]{:S(2)}) collective-permute-start(bf16[16,33,16,128]{3,2,1,0:T(8,128)(2,1)S(1)} %bitcast.30), channel_id=1, source_target_pairs={{0,1},{1,0},{2,3},{3,2},{4,5},{5,4},{6,7},{7,6},{8,9},{9,8},{10,11... | collective-permute-start | bytes 6488072 | tf_op jit(solution)/shard_map/ppermute | solution.py:366
  58.7 1.3 %copy-start = (bf16[32,128,256]{2,1,0:T(8,128)(2,1)}, bf16[32,128,256]{2,1,0:T(8,128)(2,1)S(1)}, u32[]{:S(2)}) copy-start(bf16[32,128,256]{2,1,0:T(8,128)(2,1)S(1)} %shard_map.76.own_ref) | copy-start | bytes 6291460
  74.0 1.5 %collective-permute-start.2 = (f32[8,40,128]{2,1,0:T(8,128)S(1)}, f32[8,40,128]{2,1,0:T(8,128)S(1)}, u32[]{:S(2)}, u32[]{:S(2)}) collective-permute-start(f32[8,40,128]{2,1,0:T(8,128)S(1)} %get-tuple-element.32), channel_id=1, source_target_pairs={{0,1},{1,0},{2,3},{3,2},{4,5},{5,4},{6,7},{7,6},{8,9},{9,8},{10,11... | collective-permute-start | bytes 491528 | tf_op jit(solution)/shard_map/ppermute | solution.py:391
  86.3 2.9 %collective-permute-start.3 = (f32[2,32,128]{2,1,0:T(8,128)S(1)}, f32[2,32,128]{2,1,0:T(8,128)S(1)}, u32[]{:S(2)}, u32[]{:S(2)}) collective-permute-start(f32[2,32,128]{2,1,0:T(8,128)S(1)} %log_multiply_fusion), channel_id=1, source_target_pairs={{0,1},{1,0},{2,3},{3,2},{4,5},{5,4},{6,7},{7,6},{8,9},{9,8},{10,11... | collective-permute-start | bytes 98312 | tf_op jit(solution)/shard_map/ppermute | solution.py:401
